TPU v7x, 256 devices: a whole 4x4x8 slice. The times are simulated.
256 devices in a mesh: section: 2 (over core), head: 8 (over z), seq: 16 (over y, x).
Axes of the slice: x: 4, y: 4, z: 8, core: 2. Of those that a mesh axis runs over, the one named last changes fastest.
Arguments:
- patches: bfloat16 [4, 384, 3072], P(None, 'seq', 'head'), may hold values from -6 to 6
- cache_k: bfloat16 [2, 1536, 3072], P('section', 'seq', 'head'), may hold values from -7 to 7
- cache_v: bfloat16 [2, 1536, 3072], P('section', 'seq', 'head'), may hold values from -4 to 4
- w_qkv: bfloat16 [2, 3072, 3, 3072], P('section', 'seq', None, 'head'), may hold values from -0.109375 to 0.109375
- w_out: bfloat16 [2, 3072, 3072], P('section', None, 'head'), may hold values from -0.109375 to 0.109375
- modulation: float32 [2, 3, 3072], P('section'), may hold values from -4 to 4
- qk_gain: float32 [2, 2, 128], P('section'), may hold values from 1 to 2.2
- patch_order: int32 [4], replicated, may hold values from 0 to 3, each once
- patch_start: int32 [4], replicated, may hold values from 0 to 1152, as said below
Outputs:
- block_out: bfloat16 [2, 4, 384, 3072], P('section', None, 'seq', 'head')
- new_k: bfloat16 [2, 1536, 3072], P('section', 'seq', 'head')
- new_v: bfloat16 [2, 1536, 3072], P('section', 'seq', 'head')
Inputs may be any that keep to these rules, and one draw needn't show every extreme that they name: `patch_order`: each patch appears once. Every entry is a multiple of 96; patch p covers positions patch_start[p] to patch_start[p] + 383; patches may intersect.
All inputs are finite; a program needn't handle non-finite values.
Results may differ from a plain program's by a relative error of at most 0.015.
Values may be sent and summed in bfloat16 or wider, within the bound.
A program may use at most 64 MiB of HBM per device.

v0:
```python
import math

import jax
import jax.numpy as jnp
from jax import lax
from jax.sharding import PartitionSpec as P


def passed_along(value, axis, steps):
    count = lax.axis_size(axis)
    leading, last = (max(0, -steps), min(count, count - steps))
    return lax.ppermute(value, axis, [(source, source + steps) for source in range(leading, last)])


def layer_norm(stream):
    average = jnp.mean(stream, axis=-1, keepdims=True)
    spread = jnp.mean((stream - average) ** 2, axis=-1, keepdims=True)
    return (stream - average) * lax.rsqrt(spread + 1e-06)


def rms_heads(heads_in, norm_gain):
    power = jnp.mean(heads_in * heads_in, axis=-1, keepdims=True)
    return heads_in * lax.rsqrt(power + 1e-06) * norm_gain


def head_attention(queries, key_part, value_part):
    span_len = key_part.shape[0]
    local_heads = queries.shape[1]
    head_dim = queries.shape[2]
    key_heads = key_part.reshape(span_len, local_heads, head_dim)
    val_heads = value_part.reshape(span_len, local_heads, head_dim)
    scores = jnp.einsum("qhd,khd->hqk", queries, key_heads, preferred_element_type=jnp.float32)
    weights_exp = jnp.exp(scores * (1.0 / math.sqrt(head_dim)))
    denom_sum = jnp.sum(weights_exp, axis=-1)
    numer_sum = jnp.einsum(
        "hqk,khd->qhd",
        weights_exp.astype(jnp.bfloat16),
        val_heads,
        preferred_element_type=jnp.float32,
    )
    return (numer_sum, denom_sum)


def per_device(
    patches, cache_k, cache_v, w_qkv, w_out, modulation, qk_gain, patch_order, patch_start
):
    segment_count = lax.axis_size("section")
    segment_rank = lax.axis_index("section")
    seq_rank = lax.axis_index("seq")
    head_rank = lax.axis_index("head")
    patch_count, tok_rows, feat_width = patches.shape
    shard_len = cache_k.shape[1]
    head_dim = qk_gain.shape[-1]
    local_heads = feat_width // head_dim
    full_width = w_out.shape[1]
    patch_len = tok_rows * lax.axis_size("seq")
    weights_full = lax.all_gather(w_qkv[0], "seq", axis=0, tiled=True).reshape(
        full_width, 3 * feat_width
    )
    modulate = modulation[0]
    norm_gains = qk_gain[0]
    out_rows = w_out[0]
    gate_local = lax.dynamic_slice_in_dim(modulate[2], head_rank * feat_width, feat_width)

    def run_block(stream_in, key_cache, value_cache, begin):
        full_row = lax.all_gather(stream_in, "head", axis=1, tiled=True)
        normed = (
            layer_norm(full_row.astype(jnp.float32)) * (1.0 + modulate[1]) + modulate[0]
        ).astype(jnp.bfloat16)
        projected = jnp.dot(normed, weights_full, preferred_element_type=jnp.float32)
        projected = projected.reshape(tok_rows, 3, local_heads, head_dim)
        queries = rms_heads(projected[:, 0], norm_gains[0]).astype(jnp.bfloat16)
        fresh_key = (
            rms_heads(projected[:, 1], norm_gains[1])
            .astype(jnp.bfloat16)
            .reshape(tok_rows, feat_width)
        )
        fresh_value = projected[:, 2].astype(jnp.bfloat16).reshape(tok_rows, feat_width)
        patch_keys, patch_values = (
            lax.all_gather(fresh_key, "seq", axis=0, tiled=True),
            lax.all_gather(fresh_value, "seq", axis=0, tiled=True),
        )
        my_start = seq_rank * shard_len
        inside = (my_start >= begin) & (my_start < begin + patch_len)
        offset = jnp.clip(my_start - begin, 0, patch_len - shard_len)
        new_keys = jnp.where(
            inside, lax.dynamic_slice_in_dim(patch_keys, offset, shard_len, 0), key_cache
        )
        new_values = jnp.where(
            inside, lax.dynamic_slice_in_dim(patch_values, offset, shard_len, 0), value_cache
        )
        numer_part, denom_part = head_attention(
            queries,
            lax.all_gather(new_keys, "seq", axis=0, tiled=True),
            lax.all_gather(new_values, "seq", axis=0, tiled=True),
        )
        attended = (
            (numer_part / jnp.transpose(denom_part)[:, :, None])
            .astype(jnp.bfloat16)
            .reshape(tok_rows, feat_width)
        )
        projected_out = jnp.dot(
            lax.all_gather(attended, "head", axis=1, tiled=True),
            out_rows,
            preferred_element_type=jnp.float32,
        )
        updated = (stream_in.astype(jnp.float32) + gate_local * projected_out).astype(jnp.bfloat16)
        return (updated, new_keys, new_values)

    def advance(tick_pos, state_now):
        incoming, key_cache, value_cache, collected = state_now
        order_pos = tick_pos - segment_rank
        active = (order_pos >= 0) & (order_pos < patch_count)
        slot_pos = jnp.clip(order_pos, 0, patch_count - 1)
        patch_id = patch_order[slot_pos]
        begin = patch_start[patch_id]
        fresh_input = lax.dynamic_index_in_dim(patches, patch_id, 0, keepdims=False)
        stream_in = jnp.where(segment_rank == 0, fresh_input, incoming)
        updated, next_keys, next_values = run_block(stream_in, key_cache, value_cache, begin)
        key_cache = jnp.where(active, next_keys, key_cache)
        value_cache = jnp.where(active, next_values, value_cache)
        written = lax.dynamic_update_index_in_dim(collected, updated, patch_id, 0)
        collected = jnp.where(active, written, collected)
        incoming = passed_along(updated, "section", 1)
        return (incoming, key_cache, value_cache, collected)

    start_keys, start_values = (cache_k[0], cache_v[0])
    initial_state = (
        jnp.zeros((tok_rows, feat_width), jnp.bfloat16),
        start_keys,
        start_values,
        jnp.zeros((patch_count, tok_rows, feat_width), jnp.bfloat16),
    )
    final_state = lax.fori_loop(0, patch_count + segment_count - 1, advance, initial_state)
    final_keys, final_values = (final_state[1], final_state[2])
    return (final_state[3][None], final_keys[None], final_values[None])


def solution(mesh):
    return jax.shard_map(
        per_device,
        mesh=mesh,
        in_specs=(
            P(None, "seq", "head"),
            P("section", "seq", "head"),
            P("section", "seq", "head"),
            P("section", "seq", None, "head"),
            P("section", None, "head"),
            P("section", None, None),
            P("section", None, None),
            P(),
            P(),
        ),
        out_specs=(
            P("section", None, "seq", "head"),
            P("section", "seq", "head"),
            P("section", "seq", "head"),
        ),
        check_vma=False,
    )
```

profile of v0, /device:TPU:1, one launch (start us, length us, event | category | flops | bytes accessed | tf_op | source)
XLA Modules:
  0.0 1059.7 jit_solution(3744478374589422811)
XLA Ops:
  9.4 74.8 %all-gather.5.cloned.1.call-done = bf16[1,3072,3,384]{3,1,2,0:T(8,128)(2,1)} async-done(((bf16[1,192,3,384]{3,1,2,0:T(8,128)(2,1)}), bf16[1,3072,3,384]{3,1,2,0:T(8,128)(2,1)}) %all-gather.5.cloned.1.call-update) | async-done | bytes 7077904 | tf_op jit(solution)/shard_map/all_gather | solution.py:57
  84.2 10.2 copy.29
  94.4 10.3 copy.30
  105.4 947.1 %while.21 = (s32[]{:T(128)}, bf16[24,384]{1,0:T(8,128)(2,1)S(1)}, bf16[96,384]{1,0:T(8,128)(2,1)S(1)}, bf16[96,384]{1,0:T(8,128)(2,1)S(1)}, bf16[4,24,384]{2,1,0...) while((s32[]{:T(128)}, bf16[24,384]{1,0:T(8,128)(2,1)S(1)}, ...), condition=%wide.region_6.7_spmd, body=%wide.region_0.6_spmd.sunk | while | flops 284648544 | bytes 29226860 | solution.py:134
  112.0 20.1 %all_gather.64 = bf16[24,3072]{1,0:T(8,128)(2,1)S(1)} all-gather(bf16[24,384]{1,0:T(8,128)(2,1)S(1)} %bitcast_select_fusion.3), channel_id=1, replica_groups=mesh['section'=2,'head'=8,'seq'=16] {'head'}, dimensions={1}, use_global_device_ids=true | all-gather | bytes 165888 | tf_op jit(solution)/shard_map/while/body/eval_jaxpr/all_gather | solution.py:66
  132.4 4.1 fusion.53
  136.8 18.3 %all_gather.67 = bf16[384,384]{1,0:T(8,128)(2,1)S(1)} all-gather(bf16[24,384]{1,0:T(8,128)(2,1)S(1)} %fusion.55), channel_id=1, replica_groups=mesh['section'=2,'head'=8,'seq'=16] {'seq'}, dimensions={0}, use_global_device_ids=true | all-gather | bytes 313344 | tf_op jit(solution)/shard_map/while/body/eval_jaxpr/all_gather | solution.py:80
  155.9 16.3 %all_gather.65 = bf16[384,384]{1,0:T(8,128)(2,1)S(1)} all-gather(bf16[24,384]{1,0:T(8,128)(2,1)S(1)} %bitcast.138), channel_id=1, replica_groups=mesh['section'=2,'head'=8,'seq'=16] {'seq'}, dimensions={0}, use_global_device_ids=true | all-gather | bytes 313344 | tf_op jit(solution)/shard_map/while/body/eval_jaxpr/all_gather | solution.py:81
  173.8 38.1 %all-gather.9.cloned.1.call-done = bf16[1536,384]{1,0:T(8,128)(2,1)} async-done(((bf16[96,384]{1,0:T(8,128)(2,1)}), bf16[1536,384]{1,0:T(8,128)(2,1)}) %all-gather.9.cloned.1.call-update) | async-done | bytes 1179664 | tf_op jit(solution)/shard_map/while/body/eval_jaxpr/all_gather | solution.py:94
  211.9 1.6 copy.62
  213.4 1.7 fusion.56
  215.2 47.3 %all-gather.7.cloned.1.call-done = bf16[1536,384]{1,0:T(8,128)(2,1)} async-done(((bf16[96,384]{1,0:T(8,128)(2,1)}), bf16[1536,384]{1,0:T(8,128)(2,1)}) %all-gather.7.cloned.1.call-update) | async-done | bytes 1179664 | tf_op jit(solution)/shard_map/while/body/eval_jaxpr/all_gather | solution.py:95
  262.4 1.6 copy.61
  265.4 20.2 %all_gather.69 = bf16[24,3072]{1,0:T(8,128)(2,1)S(1)} all-gather(bf16[24,384]{1,0:T(8,128)(2,1)S(1)} %bitcast.139), channel_id=1, replica_groups=mesh['section'=2,'head'=8,'seq'=16] {'head'}, dimensions={1}, use_global_device_ids=true | all-gather | bytes 165888 | tf_op jit(solution)/shard_map/while/body/eval_jaxpr/all_gather | solution.py:103
  285.6 1.8 fusion.58
  288.7 8.2 collective-permute-done
  303.5 18.3 %all_gather.64 = bf16[24,3072]{1,0:T(8,128)(2,1)S(1)} all-gather(bf16[24,384]{1,0:T(8,128)(2,1)S(1)} %bitcast_select_fusion.3), channel_id=1, replica_groups=mesh['section'=2,'head'=8,'seq'=16] {'head'}, dimensions={1}, use_global_device_ids=true | all-gather | bytes 165888 | tf_op jit(solution)/shard_map/while/body/eval_jaxpr/all_gather | solution.py:66
  322.2 4.1 fusion.53
  326.5 18.0 %all_gather.67 = bf16[384,384]{1,0:T(8,128)(2,1)S(1)} all-gather(bf16[24,384]{1,0:T(8,128)(2,1)S(1)} %fusion.55), channel_id=1, replica_groups=mesh['section'=2,'head'=8,'seq'=16] {'seq'}, dimensions={0}, use_global_device_ids=true | all-gather | bytes 313344 | tf_op jit(solution)/shard_map/while/body/eval_jaxpr/all_gather | solution.py:80
  345.3 16.2 %all_gather.65 = bf16[384,384]{1,0:T(8,128)(2,1)S(1)} all-gather(bf16[24,384]{1,0:T(8,128)(2,1)S(1)} %bitcast.138), channel_id=1, replica_groups=mesh['section'=2,'head'=8,'seq'=16] {'seq'}, dimensions={0}, use_global_device_ids=true | all-gather | bytes 313344 | tf_op jit(solution)/shard_map/while/body/eval_jaxpr/all_gather | solution.py:81
  363.0 37.8 %all-gather.9.cloned.1.call-done = bf16[1536,384]{1,0:T(8,128)(2,1)} async-done(((bf16[96,384]{1,0:T(8,128)(2,1)}), bf16[1536,384]{1,0:T(8,128)(2,1)}) %all-gather.9.cloned.1.call-update) | async-done | bytes 1179664 | tf_op jit(solution)/shard_map/while/body/eval_jaxpr/all_gather | solution.py:94
  400.8 1.6 copy.62
  402.4 1.7 fusion.56
  404.1 47.1 %all-gather.7.cloned.1.call-done = bf16[1536,384]{1,0:T(8,128)(2,1)} async-done(((bf16[96,384]{1,0:T(8,128)(2,1)}), bf16[1536,384]{1,0:T(8,128)(2,1)}) %all-gather.7.cloned.1.call-update) | async-done | bytes 1179664 | tf_op jit(solution)/shard_map/while/body/eval_jaxpr/all_gather | solution.py:95
  451.2 1.6 copy.61
  454.2 20.2 %all_gather.69 = bf16[24,3072]{1,0:T(8,128)(2,1)S(1)} all-gather(bf16[24,384]{1,0:T(8,128)(2,1)S(1)} %bitcast.139), channel_id=1, replica_groups=mesh['section'=2,'head'=8,'seq'=16] {'head'}, dimensions={1}, use_global_device_ids=true | all-gather | bytes 165888 | tf_op jit(solution)/shard_map/while/body/eval_jaxpr/all_gather | solution.py:103
  474.4 1.8 fusion.58
  477.5 8.2 collective-permute-done
  492.3 18.3 %all_gather.64 = bf16[24,3072]{1,0:T(8,128)(2,1)S(1)} all-gather(bf16[24,384]{1,0:T(8,128)(2,1)S(1)} %bitcast_select_fusion.3), channel_id=1, replica_groups=mesh['section'=2,'head'=8,'seq'=16] {'head'}, dimensions={1}, use_global_device_ids=true | all-gather | bytes 165888 | tf_op jit(solution)/shard_map/while/body/eval_jaxpr/all_gather | solution.py:66
  510.9 4.1 fusion.53
  515.3 18.0 %all_gather.67 = bf16[384,384]{1,0:T(8,128)(2,1)S(1)} all-gather(bf16[24,384]{1,0:T(8,128)(2,1)S(1)} %fusion.55), channel_id=1, replica_groups=mesh['section'=2,'head'=8,'seq'=16] {'seq'}, dimensions={0}, use_global_device_ids=true | all-gather | bytes 313344 | tf_op jit(solution)/shard_map/while/body/eval_jaxpr/all_gather | solution.py:80
  534.1 16.2 %all_gather.65 = bf16[384,384]{1,0:T(8,128)(2,1)S(1)} all-gather(bf16[24,384]{1,0:T(8,128)(2,1)S(1)} %bitcast.138), channel_id=1, replica_groups=mesh['section'=2,'head'=8,'seq'=16] {'seq'}, dimensions={0}, use_global_device_ids=true | all-gather | bytes 313344 | tf_op jit(solution)/shard_map/while/body/eval_jaxpr/all_gather | solution.py:81
  551.8 37.8 %all-gather.9.cloned.1.call-done = bf16[1536,384]{1,0:T(8,128)(2,1)} async-done(((bf16[96,384]{1,0:T(8,128)(2,1)}), bf16[1536,384]{1,0:T(8,128)(2,1)}) %all-gather.9.cloned.1.call-update) | async-done | bytes 1179664 | tf_op jit(solution)/shard_map/while/body/eval_jaxpr/all_gather | solution.py:94
  589.6 1.6 copy.62
  591.1 1.7 fusion.56
  592.9 47.3 %all-gather.7.cloned.1.call-done = bf16[1536,384]{1,0:T(8,128)(2,1)} async-done(((bf16[96,384]{1,0:T(8,128)(2,1)}), bf16[1536,384]{1,0:T(8,128)(2,1)}) %all-gather.7.cloned.1.call-update) | async-done | bytes 1179664 | tf_op jit(solution)/shard_map/while/body/eval_jaxpr/all_gather | solution.py:95
  640.1 1.6 copy.61
  643.1 20.2 %all_gather.69 = bf16[24,3072]{1,0:T(8,128)(2,1)S(1)} all-gather(bf16[24,384]{1,0:T(8,128)(2,1)S(1)} %bitcast.139), channel_id=1, replica_groups=mesh['section'=2,'head'=8,'seq'=16] {'head'}, dimensions={1}, use_global_device_ids=true | all-gather | bytes 165888 | tf_op jit(solution)/shard_map/while/body/eval_jaxpr/all_gather | solution.py:103
  663.3 1.8 fusion.58
  666.4 8.2 collective-permute-done
  681.2 18.3 %all_gather.64 = bf16[24,3072]{1,0:T(8,128)(2,1)S(1)} all-gather(bf16[24,384]{1,0:T(8,128)(2,1)S(1)} %bitcast_select_fusion.3), channel_id=1, replica_groups=mesh['section'=2,'head'=8,'seq'=16] {'head'}, dimensions={1}, use_global_device_ids=true | all-gather | bytes 165888 | tf_op jit(solution)/shard_map/while/body/eval_jaxpr/all_gather | solution.py:66
  699.9 4.1 fusion.53
  704.2 18.0 %all_gather.67 = bf16[384,384]{1,0:T(8,128)(2,1)S(1)} all-gather(bf16[24,384]{1,0:T(8,128)(2,1)S(1)} %fusion.55), channel_id=1, replica_groups=mesh['section'=2,'head'=8,'seq'=16] {'seq'}, dimensions={0}, use_global_device_ids=true | all-gather | bytes 313344 | tf_op jit(solution)/shard_map/while/body/eval_jaxpr/all_gather | solution.py:80
  723.0 16.2 %all_gather.65 = bf16[384,384]{1,0:T(8,128)(2,1)S(1)} all-gather(bf16[24,384]{1,0:T(8,128)(2,1)S(1)} %bitcast.138), channel_id=1, replica_groups=mesh['section'=2,'head'=8,'seq'=16] {'seq'}, dimensions={0}, use_global_device_ids=true | all-gather | bytes 313344 | tf_op jit(solution)/shard_map/while/body/eval_jaxpr/all_gather | solution.py:81
  740.7 37.8 %all-gather.9.cloned.1.call-done = bf16[1536,384]{1,0:T(8,128)(2,1)} async-done(((bf16[96,384]{1,0:T(8,128)(2,1)}), bf16[1536,384]{1,0:T(8,128)(2,1)}) %all-gather.9.cloned.1.call-update) | async-done | bytes 1179664 | tf_op jit(solution)/shard_map/while/body/eval_jaxpr/all_gather | solution.py:94
  778.5 1.6 copy.62
  780.1 1.7 fusion.56
  781.8 47.3 %all-gather.7.cloned.1.call-done = bf16[1536,384]{1,0:T(8,128)(2,1)} async-done(((bf16[96,384]{1,0:T(8,128)(2,1)}), bf16[1536,384]{1,0:T(8,128)(2,1)}) %all-gather.7.cloned.1.call-update) | async-done | bytes 1179664 | tf_op jit(solution)/shard_map/while/body/eval_jaxpr/all_gather | solution.py:95
  829.1 1.6 copy.61
  832.0 20.2 %all_gather.69 = bf16[24,3072]{1,0:T(8,128)(2,1)S(1)} all-gather(bf16[24,384]{1,0:T(8,128)(2,1)S(1)} %bitcast.139), channel_id=1, replica_groups=mesh['section'=2,'head'=8,'seq'=16] {'head'}, dimensions={1}, use_global_device_ids=true | all-gather | bytes 165888 | tf_op jit(solution)/shard_map/while/body/eval_jaxpr/all_gather | solution.py:103
  852.3 1.8 fusion.58
  855.3 8.2 collective-permute-done
  870.1 18.3 %all_gather.64 = bf16[24,3072]{1,0:T(8,128)(2,1)S(1)} all-gather(bf16[24,384]{1,0:T(8,128)(2,1)S(1)} %bitcast_select_fusion.3), channel_id=1, replica_groups=mesh['section'=2,'head'=8,'seq'=16] {'head'}, dimensions={1}, use_global_device_ids=true | all-gather | bytes 165888 | tf_op jit(solution)/shard_map/while/body/eval_jaxpr/all_gather | solution.py:66
  888.8 4.1 fusion.53
  893.2 18.0 %all_gather.67 = bf16[384,384]{1,0:T(8,128)(2,1)S(1)} all-gather(bf16[24,384]{1,0:T(8,128)(2,1)S(1)} %fusion.55), channel_id=1, replica_groups=mesh['section'=2,'head'=8,'seq'=16] {'seq'}, dimensions={0}, use_global_device_ids=true | all-gather | bytes 313344 | tf_op jit(solution)/shard_map/while/body/eval_jaxpr/all_gather | solution.py:80
  911.9 16.2 %all_gather.65 = bf16[384,384]{1,0:T(8,128)(2,1)S(1)} all-gather(bf16[24,384]{1,0:T(8,128)(2,1)S(1)} %bitcast.138), channel_id=1, replica_groups=mesh['section'=2,'head'=8,'seq'=16] {'seq'}, dimensions={0}, use_global_device_ids=true | all-gather | bytes 313344 | tf_op jit(solution)/shard_map/while/body/eval_jaxpr/all_gather | solution.py:81
  929.6 37.8 %all-gather.9.cloned.1.call-done = bf16[1536,384]{1,0:T(8,128)(2,1)} async-done(((bf16[96,384]{1,0:T(8,128)(2,1)}), bf16[1536,384]{1,0:T(8,128)(2,1)}) %all-gather.9.cloned.1.call-update) | async-done | bytes 1179664 | tf_op jit(solution)/shard_map/while/body/eval_jaxpr/all_gather | solution.py:94
  967.4 1.6 copy.62
  969.0 1.7 fusion.56
  970.7 47.3 %all-gather.7.cloned.1.call-done = bf16[1536,384]{1,0:T(8,128)(2,1)} async-done(((bf16[96,384]{1,0:T(8,128)(2,1)}), bf16[1536,384]{1,0:T(8,128)(2,1)}) %all-gather.7.cloned.1.call-update) | async-done | bytes 1179664 | tf_op jit(solution)/shard_map/while/body/eval_jaxpr/all_gather | solution.py:95
  1018.0 1.6 copy.61
  1021.0 20.2 %all_gather.69 = bf16[24,3072]{1,0:T(8,128)(2,1)S(1)} all-gather(bf16[24,384]{1,0:T(8,128)(2,1)S(1)} %bitcast.139), channel_id=1, replica_groups=mesh['section'=2,'head'=8,'seq'=16] {'head'}, dimensions={1}, use_global_device_ids=true | all-gather | bytes 165888 | tf_op jit(solution)/shard_map/while/body/eval_jaxpr/all_gather | solution.py:103
  1041.2 1.8 fusion.58
  1044.3 8.2 collective-permute-done
  (236 shorter events, 44.4 us)
Async XLA Ops:
  7.2 77.0 %all-gather.5.cloned.1.call-start = ((), (), s32[]{:S(2)}) async-start(), calls=%async_computation | async-start | bytes 7520256 | tf_op jit(solution)/shard_map/all_gather | solution.py:57
  94.3 11.0 %copy-start = (bf16[1,3072,384]{2,1,0:T(8,128)(2,1)S(1)}, bf16[1,3072,384]{2,1,0:T(8,128)(2,1)}, u32[]{:S(2)}) copy-start(bf16[1,3072,384]{2,1,0:T(8,128)(2,1)} %param.15) | copy-start | bytes 7077892
  94.3 11.0 %copy-start.5 = (bf16[1,96,384]{2,1,0:T(8,128)(2,1)S(1)}, bf16[1,96,384]{2,1,0:T(8,128)(2,1)}, u32[]{:S(2)}) copy-start(bf16[1,96,384]{2,1,0:T(8,128)(2,1)} %param.12) | copy-start | bytes 221188
  94.3 11.0 %copy-start.9 = (bf16[1,96,384]{2,1,0:T(8,128)(2,1)S(1)}, bf16[1,96,384]{2,1,0:T(8,128)(2,1)}, u32[]{:S(2)}) copy-start(bf16[1,96,384]{2,1,0:T(8,128)(2,1)} %param.13) | copy-start | bytes 221188
  94.3 11.0 %copy-start.12 = (f32[1,2,128]{2,1,0:T(2,128)S(1)}, f32[1,2,128]{2,1,0:T(2,128)}, u32[]{:S(2)}) copy-start(f32[1,2,128]{2,1,0:T(2,128)} %param.17) | copy-start | bytes 3076
  94.4 11.0 %copy-start.13 = (s32[4]{0:T(128)S(1)}, s32[4]{0:T(128)}, u32[]{:S(2)}) copy-start(s32[4]{0:T(128)} %param.18) | copy-start | bytes 52
  105.4 27.0 %copy-start.10 = (f32[3,3072]{1,0:T(4,128)}, f32[3,3072]{1,0:T(4,128)S(1)}, u32[]{:S(2)}) copy-start(f32[3,3072]{1,0:T(4,128)S(1)} %get-tuple-element.613) | copy-start | bytes 110596 | tf_op jit(solution)/shard_map/while
  105.4 106.5 %all-gather.9.cloned.1.call-start = ((), (), s32[]{:S(2)}) async-start(), calls=%async_computation.2 | async-start | bytes 1253376 | tf_op jit(solution)/shard_map/while/body/eval_jaxpr/all_gather | solution.py:94
  112.0 20.5 %copy-start.1 = (bf16[24,384]{1,0:T(8,128)(2,1)}, bf16[24,384]{1,0:T(8,128)(2,1)S(1)}, u32[]{:S(2)}) copy-start(bf16[24,384]{1,0:T(8,128)(2,1)S(1)} %bitcast_select_fusion.3) | copy-start | bytes 55300 | tf_op jit(solution)/shard_map/while
  155.8 18.0 %copy-start.2 = (bf16[96,384]{1,0:T(8,128)(2,1)}, bf16[96,384]{1,0:T(8,128)(2,1)S(1)}, u32[]{:S(2)}) copy-start(bf16[96,384]{1,0:T(8,128)(2,1)S(1)} %get-tuple-element.603) | copy-start | bytes 221188 | tf_op jit(solution)/shard_map/while
  155.8 106.6 %all-gather.7.cloned.1.call-start = ((), (), s32[]{:S(2)}) async-start(), calls=%async_computation.1 | async-start | bytes 1253376 | tf_op jit(solution)/shard_map/while/body/eval_jaxpr/all_gather | solution.py:95
  172.9 0.8 copy-start.6
  265.4 31.6 %copy-start.3 = (bf16[96,384]{1,0:T(8,128)(2,1)S(1)}, bf16[96,384]{1,0:T(8,128)(2,1)}, u32[]{:S(2)}) copy-start(bf16[96,384]{1,0:T(8,128)(2,1)} %copy-done.2) | copy-start | bytes 221188 | tf_op jit(solution)/shard_map/while
  265.4 31.6 %copy-start.7 = (bf16[96,384]{1,0:T(8,128)(2,1)S(1)}, bf16[96,384]{1,0:T(8,128)(2,1)}, u32[]{:S(2)}) copy-start(bf16[96,384]{1,0:T(8,128)(2,1)} %copy-done.6) | copy-start | bytes 221188 | tf_op jit(solution)/shard_map/while
  265.4 31.5 %copy-start.11 = (f32[3,3072]{1,0:T(4,128)S(1)}, f32[3,3072]{1,0:T(4,128)}, u32[]{:S(2)}) copy-start(f32[3,3072]{1,0:T(4,128)} %copy-done.10) | copy-start | bytes 110596 | tf_op jit(solution)/shard_map/while
  287.4 9.5 collective-permute-start
  296.9 25.2 %copy-start.10 = (f32[3,3072]{1,0:T(4,128)}, f32[3,3072]{1,0:T(4,128)S(1)}, u32[]{:S(2)}) copy-start(f32[3,3072]{1,0:T(4,128)S(1)} %get-tuple-element.613) | copy-start | bytes 110596 | tf_op jit(solution)/shard_map/while
  296.9 103.9 %all-gather.9.cloned.1.call-start = ((), (), s32[]{:S(2)}) async-start(), calls=%async_computation.2 | async-start | bytes 1253376 | tf_op jit(solution)/shard_map/while/body/eval_jaxpr/all_gather | solution.py:94
  303.5 18.6 %copy-start.1 = (bf16[24,384]{1,0:T(8,128)(2,1)}, bf16[24,384]{1,0:T(8,128)(2,1)S(1)}, u32[]{:S(2)}) copy-start(bf16[24,384]{1,0:T(8,128)(2,1)S(1)} %bitcast_select_fusion.3) | copy-start | bytes 55300 | tf_op jit(solution)/shard_map/while
  345.2 17.8 %copy-start.2 = (bf16[96,384]{1,0:T(8,128)(2,1)}, bf16[96,384]{1,0:T(8,128)(2,1)S(1)}, u32[]{:S(2)}) copy-start(bf16[96,384]{1,0:T(8,128)(2,1)S(1)} %get-tuple-element.603) | copy-start | bytes 221188 | tf_op jit(solution)/shard_map/while
  345.2 106.0 %all-gather.7.cloned.1.call-start = ((), (), s32[]{:S(2)}) async-start(), calls=%async_computation.1 | async-start | bytes 1253376 | tf_op jit(solution)/shard_map/while/body/eval_jaxpr/all_gather | solution.py:95
  362.2 0.8 copy-start.6
  454.1 31.6 %copy-start.3 = (bf16[96,384]{1,0:T(8,128)(2,1)S(1)}, bf16[96,384]{1,0:T(8,128)(2,1)}, u32[]{:S(2)}) copy-start(bf16[96,384]{1,0:T(8,128)(2,1)} %copy-done.2) | copy-start | bytes 221188 | tf_op jit(solution)/shard_map/while
  454.1 31.6 %copy-start.7 = (bf16[96,384]{1,0:T(8,128)(2,1)S(1)}, bf16[96,384]{1,0:T(8,128)(2,1)}, u32[]{:S(2)}) copy-start(bf16[96,384]{1,0:T(8,128)(2,1)} %copy-done.6) | copy-start | bytes 221188 | tf_op jit(solution)/shard_map/while
  454.2 31.5 %copy-start.11 = (f32[3,3072]{1,0:T(4,128)S(1)}, f32[3,3072]{1,0:T(4,128)}, u32[]{:S(2)}) copy-start(f32[3,3072]{1,0:T(4,128)} %copy-done.10) | copy-start | bytes 110596 | tf_op jit(solution)/shard_map/while
  476.2 9.5 collective-permute-start
  485.7 25.2 %copy-start.10 = (f32[3,3072]{1,0:T(4,128)}, f32[3,3072]{1,0:T(4,128)S(1)}, u32[]{:S(2)}) copy-start(f32[3,3072]{1,0:T(4,128)S(1)} %get-tuple-element.613) | copy-start | bytes 110596 | tf_op jit(solution)/shard_map/while
  485.7 103.9 %all-gather.9.cloned.1.call-start = ((), (), s32[]{:S(2)}) async-start(), calls=%async_computation.2 | async-start | bytes 1253376 | tf_op jit(solution)/shard_map/while/body/eval_jaxpr/all_gather | solution.py:94
  492.3 18.6 %copy-start.1 = (bf16[24,384]{1,0:T(8,128)(2,1)}, bf16[24,384]{1,0:T(8,128)(2,1)S(1)}, u32[]{:S(2)}) copy-start(bf16[24,384]{1,0:T(8,128)(2,1)S(1)} %bitcast_select_fusion.3) | copy-start | bytes 55300 | tf_op jit(solution)/shard_map/while
  534.0 17.8 %copy-start.2 = (bf16[96,384]{1,0:T(8,128)(2,1)}, bf16[96,384]{1,0:T(8,128)(2,1)S(1)}, u32[]{:S(2)}) copy-start(bf16[96,384]{1,0:T(8,128)(2,1)S(1)} %get-tuple-element.603) | copy-start | bytes 221188 | tf_op jit(solution)/shard_map/while
  534.0 106.1 %all-gather.7.cloned.1.call-start = ((), (), s32[]{:S(2)}) async-start(), calls=%async_computation.1 | async-start | bytes 1253376 | tf_op jit(solution)/shard_map/while/body/eval_jaxpr/all_gather | solution.py:95
  550.9 0.8 copy-start.6
  643.0 31.6 %copy-start.3 = (bf16[96,384]{1,0:T(8,128)(2,1)S(1)}, bf16[96,384]{1,0:T(8,128)(2,1)}, u32[]{:S(2)}) copy-start(bf16[96,384]{1,0:T(8,128)(2,1)} %copy-done.2) | copy-start | bytes 221188 | tf_op jit(solution)/shard_map/while
  643.0 31.6 %copy-start.7 = (bf16[96,384]{1,0:T(8,128)(2,1)S(1)}, bf16[96,384]{1,0:T(8,128)(2,1)}, u32[]{:S(2)}) copy-start(bf16[96,384]{1,0:T(8,128)(2,1)} %copy-done.6) | copy-start | bytes 221188 | tf_op jit(solution)/shard_map/while
  643.1 31.5 %copy-start.11 = (f32[3,3072]{1,0:T(4,128)S(1)}, f32[3,3072]{1,0:T(4,128)}, u32[]{:S(2)}) copy-start(f32[3,3072]{1,0:T(4,128)} %copy-done.10) | copy-start | bytes 110596 | tf_op jit(solution)/shard_map/while
  665.1 9.5 collective-permute-start
  674.6 25.2 %copy-start.10 = (f32[3,3072]{1,0:T(4,128)}, f32[3,3072]{1,0:T(4,128)S(1)}, u32[]{:S(2)}) copy-start(f32[3,3072]{1,0:T(4,128)S(1)} %get-tuple-element.613) | copy-start | bytes 110596 | tf_op jit(solution)/shard_map/while
  674.6 103.9 %all-gather.9.cloned.1.call-start = ((), (), s32[]{:S(2)}) async-start(), calls=%async_computation.2 | async-start | bytes 1253376 | tf_op jit(solution)/shard_map/while/body/eval_jaxpr/all_gather | solution.py:94
  681.2 18.6 %copy-start.1 = (bf16[24,384]{1,0:T(8,128)(2,1)}, bf16[24,384]{1,0:T(8,128)(2,1)S(1)}, u32[]{:S(2)}) copy-start(bf16[24,384]{1,0:T(8,128)(2,1)S(1)} %bitcast_select_fusion.3) | copy-start | bytes 55300 | tf_op jit(solution)/shard_map/while
  722.9 17.8 %copy-start.2 = (bf16[96,384]{1,0:T(8,128)(2,1)}, bf16[96,384]{1,0:T(8,128)(2,1)S(1)}, u32[]{:S(2)}) copy-start(bf16[96,384]{1,0:T(8,128)(2,1)S(1)} %get-tuple-element.603) | copy-start | bytes 221188 | tf_op jit(solution)/shard_map/while
  722.9 106.1 %all-gather.7.cloned.1.call-start = ((), (), s32[]{:S(2)}) async-start(), calls=%async_computation.1 | async-start | bytes 1253376 | tf_op jit(solution)/shard_map/while/body/eval_jaxpr/all_gather | solution.py:95
  739.8 0.8 copy-start.6
  832.0 31.6 %copy-start.3 = (bf16[96,384]{1,0:T(8,128)(2,1)S(1)}, bf16[96,384]{1,0:T(8,128)(2,1)}, u32[]{:S(2)}) copy-start(bf16[96,384]{1,0:T(8,128)(2,1)} %copy-done.2) | copy-start | bytes 221188 | tf_op jit(solution)/shard_map/while
  832.0 31.6 %copy-start.7 = (bf16[96,384]{1,0:T(8,128)(2,1)S(1)}, bf16[96,384]{1,0:T(8,128)(2,1)}, u32[]{:S(2)}) copy-start(bf16[96,384]{1,0:T(8,128)(2,1)} %copy-done.6) | copy-start | bytes 221188 | tf_op jit(solution)/shard_map/while
  832.0 31.5 %copy-start.11 = (f32[3,3072]{1,0:T(4,128)S(1)}, f32[3,3072]{1,0:T(4,128)}, u32[]{:S(2)}) copy-start(f32[3,3072]{1,0:T(4,128)} %copy-done.10) | copy-start | bytes 110596 | tf_op jit(solution)/shard_map/while
  854.1 9.5 collective-permute-start
  863.5 25.2 %copy-start.10 = (f32[3,3072]{1,0:T(4,128)}, f32[3,3072]{1,0:T(4,128)S(1)}, u32[]{:S(2)}) copy-start(f32[3,3072]{1,0:T(4,128)S(1)} %get-tuple-element.613) | copy-start | bytes 110596 | tf_op jit(solution)/shard_map/while
  863.6 103.9 %all-gather.9.cloned.1.call-start = ((), (), s32[]{:S(2)}) async-start(), calls=%async_computation.2 | async-start | bytes 1253376 | tf_op jit(solution)/shard_map/while/body/eval_jaxpr/all_gather | solution.py:94
  870.1 18.6 %copy-start.1 = (bf16[24,384]{1,0:T(8,128)(2,1)}, bf16[24,384]{1,0:T(8,128)(2,1)S(1)}, u32[]{:S(2)}) copy-start(bf16[24,384]{1,0:T(8,128)(2,1)S(1)} %bitcast_select_fusion.3) | copy-start | bytes 55300 | tf_op jit(solution)/shard_map/while
  911.8 17.8 %copy-start.2 = (bf16[96,384]{1,0:T(8,128)(2,1)}, bf16[96,384]{1,0:T(8,128)(2,1)S(1)}, u32[]{:S(2)}) copy-start(bf16[96,384]{1,0:T(8,128)(2,1)S(1)} %get-tuple-element.603) | copy-start | bytes 221188 | tf_op jit(solution)/shard_map/while
  911.9 106.1 %all-gather.7.cloned.1.call-start = ((), (), s32[]{:S(2)}) async-start(), calls=%async_computation.1 | async-start | bytes 1253376 | tf_op jit(solution)/shard_map/while/body/eval_jaxpr/all_gather | solution.py:95
  928.8 0.8 copy-start.6
  1020.9 31.6 %copy-start.3 = (bf16[96,384]{1,0:T(8,128)(2,1)S(1)}, bf16[96,384]{1,0:T(8,128)(2,1)}, u32[]{:S(2)}) copy-start(bf16[96,384]{1,0:T(8,128)(2,1)} %copy-done.2) | copy-start | bytes 221188 | tf_op jit(solution)/shard_map/while
  1020.9 31.6 %copy-start.7 = (bf16[96,384]{1,0:T(8,128)(2,1)S(1)}, bf16[96,384]{1,0:T(8,128)(2,1)}, u32[]{:S(2)}) copy-start(bf16[96,384]{1,0:T(8,128)(2,1)} %copy-done.6) | copy-start | bytes 221188 | tf_op jit(solution)/shard_map/while
  1020.9 31.5 %copy-start.11 = (f32[3,3072]{1,0:T(4,128)S(1)}, f32[3,3072]{1,0:T(4,128)}, u32[]{:S(2)}) copy-start(f32[3,3072]{1,0:T(4,128)} %copy-done.10) | copy-start | bytes 110596 | tf_op jit(solution)/shard_map/while
  1043.0 9.5 collective-permute-start
  1052.5 0.6 copy-start.4
  1052.5 0.6 copy-start.8
Sparse Core Ops, SparseCore 0:
  10.4 73.7 all-gather.4
  155.9 55.8 all-gather.8
  214.9 47.5 all-gather.6
  345.4 55.3 all-gather.8
  403.6 47.5 all-gather.6
  534.1 55.3 all-gather.8
  592.6 47.5 all-gather.6
  723.0 55.3 all-gather.8
  781.5 47.5 all-gather.6
  912.0 55.3 all-gather.8
  970.4 47.5 all-gather.6
where the time goes:
time: 1060 us
  waiting for transfers between devices  542 us (51%)
  blocking collectives  365 us (34%)
  local copies, waits for them, and re-layouts  49.1 us (5%)
  matrix products  44.8 us (4%)
  loops' own time  20.7 us (2%)
  other arithmetic  17 us (2%)
  between operations  13.8 us (1%)
    all_gather x5, waiting for transfers between devices, run_block(): lax.all_gather(new_values, 'seq', axis=0, tiled=True)  236 us
    all_gather x5, waiting for transfers between devices, run_block(): lax.all_gather(new_keys, 'seq', axis=0, tiled=True)  189 us
    all_gather x5, blocking collectives, run_block(): lax.all_gather(attended, 'head', axis=1, tiled=True)  101 us
    all_gather x5, blocking collectives, run_block(): full_row = lax.all_gather(stream_in, 'head', axis=1, tiled=True)  93.1 us
    all_gather x5, blocking collectives, run_block(): lax.all_gather(fresh_key, 'seq', axis=0, tiled=True)  90.2 us
    all_gather x5, blocking collectives, run_block(): lax.all_gather(fresh_value, 'seq', axis=0, tiled=True)  81 us
    all_gather x1, waiting for transfers between devices, per_device(): lax.all_gather(w_qkv[0], 'seq', axis=0, tiled=True)  74.8 us
    ppermute x5, waiting for transfers between devices, passed_along(): lax.ppermute(value, axis, [(source, source + steps) for source in range(l...  40.9 us
  transfers between devices with their start and end apart: 16, of which 16 were waited for; matrix products, arithmetic and copies ran while one was open for 2% of the time, Pallas kernels for 0%

commit v1 on v0

v1 whole, which is shorter than its diff:
```python
import functools
import math

import jax
import jax.numpy as jnp
from jax import lax
from jax.experimental import pallas as pl
from jax.experimental.pallas import tpu as pltpu
from jax.sharding import PartitionSpec as P

MESH = pl.DeviceIdType.MESH
F32 = jnp.float32
BF16 = jnp.bfloat16
FAR = -1e30


def square_side(count):
    side = math.isqrt(count)
    assert side * side == count
    return side


def block_kernel(
    nz,
    ny,
    nx,
    patches,
    tok,
    head_dim,
    order,
    start,
    x_in,
    ck,
    cv,
    w,
    wo,
    mod,
    gain,
    bo,
    nk,
    nv,
    xg,
    ns,
    xe,
    wbuf,
    wo_v,
    psend,
    precv,
    qg,
    kall,
    vall,
    bias,
    tag,
    nsend,
    nrecv,
    ag,
    rsend,
    rrecv,
    loc,
    xg_s,
    xg_r,
    ns_s,
    xe_r,
    w_s,
    w_r,
    c_s,
    c_r,
    p_s,
    p_r,
    q_s,
    q_r,
    kv_s,
    kv_r,
    n_s,
    n_r,
    ag_s,
    ag_r,
    r_s,
    r_r,
    hand_s,
    hand_r,
    go,
):
    sec = lax.axis_index("section")
    z = lax.axis_index("head")
    seq = lax.axis_index("seq")
    y = seq // nx
    x = lax.rem(seq, nx)
    rows, feat = x_in.shape
    chunk = ck.shape[0]
    heads = feat // head_dim
    width = nz * feat
    w_rows = w.shape[1]
    hz = nz // ny
    fresh = ny * rows
    span = ny * chunk
    pad = rrecv.shape[2]

    def on_z(d):
        return (sec, lax.rem(z + d, nz), seq)

    def on_y(d):
        return (sec, z, lax.rem(y + d, ny) * nx + x)

    def on_x(d):
        return (sec, z, y * nx + lax.rem(x + d, nx))

    other = (1 - sec, z, seq)

    def z_at(d):
        return lax.rem(z + d, nz)

    def y_at(d):
        return lax.rem(y + d, ny)

    def x_at(d):
        return lax.rem(x + d, nx)

    def copy(src, dst, ss, rs, dev):
        return pltpu.make_async_remote_copy(
            src_ref=src, dst_ref=dst, send_sem=ss, recv_sem=rs, device_id=dev, device_id_type=MESH
        )

    def arrived(dst, rs):
        copy(dst, dst, rs, rs, other).wait_recv()

    barrier = pltpu.get_barrier_semaphore()
    partners = (
        [on_z(d) for d in range(1, nz)]
        + [on_y(d) for d in range(1, ny)]
        + [on_x(d) for d in range(1, nx)]
        + [other]
    )
    for dev in partners:
        pl.semaphore_signal(barrier, inc=1, device_id=dev, device_id_type=MESH)
    pl.semaphore_wait(barrier, len(partners))

    my_w_rows = pl.ds(pl.multiple_of(x * w_rows, w_rows), w_rows)
    my_cache = pl.ds(pl.multiple_of(fresh + y * chunk, chunk), chunk)
    local = [
        pltpu.make_async_copy(w, wbuf.at[:, my_w_rows, :], loc.at[0]),
        pltpu.make_async_copy(ck, kall.at[my_cache, :], loc.at[1]),
        pltpu.make_async_copy(cv, vall.at[my_cache, :], loc.at[2]),
        pltpu.make_async_copy(wo, wo_v, loc.at[3]),
    ]

    hand = copy(bo, xg.at[z], hand_s, hand_r, other)
    z_copies = [copy(xg.at[z], xg.at[z], xg_s.at[d], xg_r.at[z], on_z(d)) for d in range(1, nz)]
    w_copies = [
        copy(w, wbuf.at[:, my_w_rows, :], w_s.at[d], w_r.at[x], on_x(d)) for d in range(1, nx)
    ]
    cache_copies = [
        copy(src, dst.at[my_cache, :], c_s.at[i, d], c_r.at[i, y], on_y(d))
        for d in range(1, ny)
        for i, (src, dst) in enumerate(((ck, kall), (cv, vall)))
    ]
    n_copies = [copy(ns.at[d], xe.at[y], ns_s.at[d], xe_r.at[y], on_y(d)) for d in range(1, ny)]
    p_copies = [
        [
            copy(psend.at[i, y_at(d)], precv.at[i, y], p_s.at[i, d], p_r.at[i, y], on_y(d))
            for d in range(1, ny)
        ]
        for i in range(3)
    ]
    q_copies = [copy(qg.at[x], qg.at[x], q_s.at[d], q_r.at[x], on_x(d)) for d in range(1, nx)]
    my_fresh = pl.ds(pl.multiple_of(y * rows, rows), rows)
    kv_copies = [
        [
            copy(
                ref.at[my_fresh, :], ref.at[my_fresh, :], kv_s.at[i, d], kv_r.at[i, y], on_y(d)
            )
            for d in range(1, ny)
        ]
        for i, ref in enumerate((kall, vall))
    ]
    num_copies = [
        copy(nsend.at[x_at(d)], nrecv.at[x], n_s.at[d], n_r.at[x], on_x(d)) for d in range(1, nx)
    ]
    a_copies = [copy(ag.at[z], ag.at[z], ag_s.at[d], ag_r.at[z], on_z(d)) for d in range(1, nz)]
    r_copies = [
        copy(rsend.at[i, x_at(d)], rrecv.at[i, x], r_s.at[i, d], r_r.at[i, x], on_x(d))
        for d in range(1, nx)
        for i in range(2)
    ]

    @pl.when(sec == 0)
    def _():
        xg[z] = x_in[...]
        for c in z_copies + w_copies:
            c.start()

    for c in local:
        c.start()

    @pl.when(sec == 1)
    def _():
        pl.semaphore_wait(go.at[0], 1)
        for c in w_copies:
            c.start()
        pl.semaphore_wait(go.at[1], 1)
        for c in cache_copies:
            c.start()

    places = [order[i] for i in range(patches)]
    begins = [start[i] for i in range(patches)]
    steps = [
        sum(jnp.where(places[s] == p, s, 0) for s in range(patches)) for p in range(patches)
    ]

    def first_after(step, pos):
        found = patches
        for p in range(patches):
            hit = (steps[p] > step) & (begins[p] <= pos) & (pos < begins[p] + span)
            found = jnp.where(hit, jnp.minimum(found, steps[p]), found)
        return found

    lane = lax.broadcasted_iota(jnp.int32, (tok, head_dim), 1)
    lane_chunk = lax.broadcasted_iota(jnp.int32, (chunk, head_dim), 1)
    for j in range(ny):
        parts = []
        for p in range(patches):
            upto = first_after(steps[p], begins[p] + j * chunk)
            parts.append(jnp.where((lane >= steps[p]) & (lane < upto), 0.0, FAR))
        bias[j * rows : (j + 1) * rows, :] = jnp.concatenate(parts, axis=0).astype(BF16)
        upto = first_after(-1, (j * nx + x) * chunk)
        bias[fresh + j * chunk : fresh + (j + 1) * chunk, :] = jnp.where(
            lane_chunk < upto, 0.0, FAR
        ).astype(BF16)
    tag[...] = jnp.concatenate(
        [jnp.where(lane == steps[p], 1.0, 0.0) for p in range(patches)], axis=0
    ).astype(BF16)

    @pl.when(sec == 1)
    def _():
        arrived(xg.at[z], hand_r)
        for c in z_copies:
            c.start()

    for d in range(1, nz):
        arrived(xg.at[z_at(d)], xg_r.at[z_at(d)])
    total = jnp.zeros((rows, feat), F32)
    for i in range(nz):
        total += xg[i].astype(F32)
    mean = jnp.sum(total, axis=-1, keepdims=True) * (1.0 / width)
    total = jnp.zeros((rows, feat), F32)
    for i in range(nz):
        diff = xg[i].astype(F32) - mean
        total += diff * diff
    spread = jnp.sum(total, axis=-1, keepdims=True) * (1.0 / width)
    scale = lax.rsqrt(spread + 1e-06)

    def normed(i):
        at = pl.ds(pl.multiple_of(i * feat, feat), feat)
        value = (xg[i].astype(F32) - mean) * scale * (1.0 + mod[1, :, at]) + mod[0, :, at]
        return value.astype(BF16)

    for d in list(range(1, ny)) + [0]:
        for i in range(hz):
            value = normed(y_at(d) * hz + i)
            if d:
                ns[d, :, i * feat : (i + 1) * feat] = value
            else:
                xe[y, :, i * feat : (i + 1) * feat] = value
        if d:
            n_copies[d - 1].start()

    @pl.when(sec == 0)
    def _():
        for c in cache_copies:
            c.start()

    local[0].wait()
    for d in range(1, nx):
        at = pl.ds(pl.multiple_of(x_at(d) * w_rows, w_rows), w_rows)
        arrived(wbuf.at[:, at, :], w_r.at[x_at(d)])

    @pl.when(sec == 0)
    def _():
        pl.semaphore_signal(go.at[0], inc=1, device_id=other, device_id_type=MESH)

    for d in range(1, ny):
        arrived(xe.at[y_at(d)], xe_r.at[y_at(d)])
    tokens = xe[...].reshape(ny * rows, hz * feat)
    for i in (1, 0, 2):
        value = jnp.dot(tokens, wbuf[i], preferred_element_type=F32)
        psend[i] = value.astype(BF16).reshape(ny, rows, feat)
        for c in p_copies[i]:
            c.start()

    def projected(i):
        value = psend[i, y].astype(F32)
        for d in range(1, ny):
            arrived(precv.at[i, y_at(d)], p_r.at[i, y_at(d)])
            value += precv[i, y_at(d)].astype(F32)
        return value

    def rms_heads(value, which):
        out = []
        for h in range(heads):
            part = value[:, h * head_dim : (h + 1) * head_dim]
            power = jnp.sum(part * part, axis=-1, keepdims=True) * (1.0 / head_dim)
            out.append(part * lax.rsqrt(power + 1e-06) * gain[which : which + 1, :])
        return jnp.concatenate(out, axis=-1).astype(BF16)

    kall[my_fresh, :] = rms_heads(projected(1), 1)
    for c in kv_copies[0]:
        c.start()
    qg[x] = rms_heads(projected(0), 0)
    for c in q_copies:
        c.start()
    vall[my_fresh, :] = projected(2).astype(BF16)
    for c in kv_copies[1]:
        c.start()

    for i, ref in enumerate((kall, vall)):
        local[1 + i].wait()
        for d in range(1, ny):
            at = pl.ds(pl.multiple_of(fresh + y_at(d) * chunk, chunk), chunk)
            arrived(ref.at[at, :], c_r.at[i, y_at(d)])
    for i, ref in enumerate((kall, vall)):
        for d in range(1, ny):
            at = pl.ds(pl.multiple_of(y_at(d) * rows, rows), rows)
            arrived(ref.at[at, :], kv_r.at[i, y_at(d)])
    for d in range(1, nx):
        arrived(qg.at[x_at(d)], q_r.at[x_at(d)])

    @pl.when(sec == 0)
    def _():
        pl.semaphore_signal(go.at[1], inc=1, device_id=other, device_id_type=MESH)

    tags = jnp.concatenate([tag[...]] * nx, axis=0)
    lane_all = lax.broadcasted_iota(jnp.int32, (nx * rows, head_dim), 1)
    sums = jnp.zeros((nx * rows, head_dim), F32)
    exponent = math.log2(math.e) / math.sqrt(head_dim)
    for h in range(heads):
        at = slice(h * head_dim, (h + 1) * head_dim)
        queries = jnp.concatenate([qg[:, :, at].reshape(nx * rows, head_dim), tags], axis=1)
        keys = jnp.concatenate([kall[:, at], bias[...]], axis=1)
        scores = lax.dot_general(
            queries, keys, (((1,), (1,)), ((), ())), preferred_element_type=F32
        )
        weight = jnp.exp2(scores * exponent)
        denom = jnp.sum(weight, axis=-1, keepdims=True)
        numer = jnp.dot(weight.astype(BF16), vall[:, at], preferred_element_type=F32)
        nsend[:, :, at] = numer.astype(BF16).reshape(nx, rows, head_dim)
        high = denom.astype(BF16).astype(F32)
        sums = jnp.where(lane_all == 2 * h, high, sums)
        sums = jnp.where(lane_all == 2 * h + 1, denom - high, sums)
    nsend[:, :, feat:] = sums.astype(BF16).reshape(nx, rows, head_dim)
    for c in num_copies:
        c.start()

    def source(c):
        pos = c * chunk
        last = -1
        first_row = -fresh - pad
        for p in range(patches):
            hit = (begins[p] <= pos) & (pos < begins[p] + span) & (steps[p] > last)
            last = jnp.where(hit, steps[p], last)
            row = (pos - begins[p]) // chunk * rows + p * tok
            first_row = jnp.where(hit, row, first_row)
        return first_row, last

    in_row = lax.broadcasted_iota(jnp.int32, (pad, fresh), 0)
    in_col = lax.broadcasted_iota(jnp.int32, (pad, fresh), 1)
    picks = []
    for c in range(nx):
        first_row, _ = source(y * nx + c)
        hit = (in_col - in_row == first_row) & (in_row < tok)
        picks.append(jnp.where(hit, 1.0, 0.0).astype(BF16))
    pick = jnp.concatenate(picks, axis=0)
    for i, ref in enumerate((kall, vall)):
        value = jnp.dot(pick, ref[0:fresh, :], preferred_element_type=F32)
        rsend[i] = value.astype(BF16).reshape(nx, pad, feat)
    for c in r_copies:
        c.start()

    numer = nsend[x, :, 0:feat].astype(F32)
    denom = nsend[x, :, feat:].astype(F32)
    for d in range(1, nx):
        arrived(nrecv.at[x_at(d)], n_r.at[x_at(d)])
        numer += nrecv[x_at(d), :, 0:feat].astype(F32)
        denom += nrecv[x_at(d), :, feat:].astype(F32)
    attended = []
    for h in range(heads):
        part = numer[:, h * head_dim : (h + 1) * head_dim]
        attended.append(part / (denom[:, 2 * h : 2 * h + 1] + denom[:, 2 * h + 1 : 2 * h + 2]))
    ag[z] = jnp.concatenate(attended, axis=-1).astype(BF16)
    for c in a_copies:
        c.start()

    local[3].wait()
    result = jnp.zeros((rows, feat), F32)
    for d in range(nz):
        i = z_at(d)
        if d:
            arrived(ag.at[i], ag_r.at[i])
        at = pl.ds(pl.multiple_of(i * feat, feat), feat)
        result += jnp.dot(ag[i], wo_v[at, :], preferred_element_type=F32)
    gate = mod[2, :, pl.ds(pl.multiple_of(z * feat, feat), feat)]
    bo[...] = (xg[z].astype(F32) + gate * result).astype(BF16)

    @pl.when(sec == 0)
    def _():
        hand.start()

    for i in range(2):
        for d in range(1, nx):
            arrived(rrecv.at[i, x_at(d)], r_r.at[i, x_at(d)])
        rrecv[i, x] = rsend[i, x]
    out_row = lax.broadcasted_iota(jnp.int32, (chunk, nx * pad), 0)
    out_col = lax.broadcasted_iota(jnp.int32, (chunk, nx * pad), 1)
    block = out_col // pad
    within = out_col - block * pad
    hit = (out_row == block * tok + within) & (within < tok)
    place = jnp.where(hit, 1.0, 0.0).astype(BF16)
    _, last = source(seq)
    for i, (old, new) in enumerate(((kall, nk), (vall, nv))):
        value = jnp.dot(place, rrecv[i].reshape(nx * pad, feat), preferred_element_type=F32)
        new[...] = jnp.where(last >= 0, value, old[my_cache, :].astype(F32)).astype(BF16)

    @pl.when(sec == 0)
    def _():
        hand.wait_send()

    for c in z_copies + w_copies + cache_copies + n_copies + q_copies + num_copies:
        c.wait_send()
    for c in sum(p_copies, []) + sum(kv_copies, []) + a_copies + r_copies:
        c.wait_send()


def per_device(
    patches, cache_k, cache_v, w_qkv, w_out, modulation, qk_gain, patch_order, patch_start
):
    nz = lax.axis_size("head")
    ny = nx = square_side(lax.axis_size("seq"))
    count, tok, feat = patches.shape
    chunk = cache_k.shape[1]
    head_dim = qk_gain.shape[-1]
    rows = count * tok
    hz = nz // ny
    width = nz * feat
    w_rows = w_qkv.shape[1]
    pad = -(-tok // 16) * 16
    keys = ny * (rows + chunk)
    dma = pltpu.SemaphoreType.DMA
    vmem = pl.BlockSpec(memory_space=pltpu.VMEM)
    smem = pl.BlockSpec(memory_space=pltpu.SMEM)
    hbm = pl.BlockSpec(memory_space=pl.ANY)
    out, new_k, new_v = pl.pallas_call(
        functools.partial(block_kernel, nz, ny, nx, count, tok, head_dim),
        name="blocks",
        out_shape=(
            jax.ShapeDtypeStruct((rows, feat), BF16),
            jax.ShapeDtypeStruct((chunk, feat), BF16),
            jax.ShapeDtypeStruct((chunk, feat), BF16),
        ),
        in_specs=[smem, smem, vmem, vmem, vmem, hbm, hbm, vmem, vmem],
        out_specs=(vmem, vmem, vmem),
        scratch_shapes=[
            pltpu.VMEM((nz, rows, feat), BF16),
            pltpu.VMEM((ny, rows, hz * feat), BF16),
            pltpu.VMEM((ny, rows, hz * feat), BF16),
            pltpu.VMEM((3, nx * w_rows, feat), BF16),
            pltpu.VMEM((width, feat), BF16),
            pltpu.VMEM((3, ny, rows, feat), BF16),
            pltpu.VMEM((3, ny, rows, feat), BF16),
            pltpu.VMEM((nx, rows, feat), BF16),
            pltpu.VMEM((keys, feat), BF16),
            pltpu.VMEM((keys, feat), BF16),
            pltpu.VMEM((keys, head_dim), BF16),
            pltpu.VMEM((rows, head_dim), BF16),
            pltpu.VMEM((nx, rows, feat + head_dim), BF16),
            pltpu.VMEM((nx, rows, feat + head_dim), BF16),
            pltpu.VMEM((nz, rows, feat), BF16),
            pltpu.VMEM((2, nx, pad, feat), BF16),
            pltpu.VMEM((2, nx, pad, feat), BF16),
            dma((4,)),
            dma((nz,)),
            dma((nz,)),
            dma((ny,)),
            dma((ny,)),
            dma((nx,)),
            dma((nx,)),
            dma((2, ny)),
            dma((2, ny)),
            dma((3, ny)),
            dma((3, ny)),
            dma((nx,)),
            dma((nx,)),
            dma((2, ny)),
            dma((2, ny)),
            dma((nx,)),
            dma((nx,)),
            dma((nz,)),
            dma((nz,)),
            dma((2, nx)),
            dma((2, nx)),
            dma,
            dma,
            pltpu.SemaphoreType.REGULAR((2,)),
        ],
        compiler_params=pltpu.CompilerParams(
            collective_id=0, has_side_effects=True, vmem_limit_bytes=48 << 20
        ),
    )(
        patch_order,
        patch_start,
        patches.reshape(rows, feat),
        cache_k[0],
        cache_v[0],
        jnp.transpose(w_qkv[0], (1, 0, 2)),
        w_out[0],
        jnp.transpose(modulation, (1, 0, 2)),
        qk_gain[0],
    )
    return (out.reshape(1, count, tok, feat), new_k[None], new_v[None])


def solution(mesh):
    return jax.shard_map(
        per_device,
        mesh=mesh,
        in_specs=(
            P(None, "seq", "head"),
            P("section", "seq", "head"),
            P("section", "seq", "head"),
            P("section", "seq", None, "head"),
            P("section", None, "head"),
            P("section", None, None),
            P("section", None, None),
            P(),
            P(),
        ),
        out_specs=(
            P("section", None, "seq", "head"),
            P("section", "seq", "head"),
            P("section", "seq", "head"),
        ),
        check_vma=False,
    )
```

time: 1060 us -> 114 us (0.11)
  waiting for transfers between devices: 542 us -> 0 us
  blocking collectives: 365 us -> 0 us
  Pallas kernels: 0 us -> 103 us
  matrix products: 44.8 us -> 0 us
  local copies, waits for them, and re-layouts: 49.1 us -> 9.98 us
  loops' own time: 20.7 us -> 0 us
  other arithmetic: 17 us -> 0 us
  between operations: 13.8 us -> 0.66 us
    all_gather x11 -> x0, waiting for transfers between devices: 500 us -> none  [the longest x5 236 us: run_block(): lax.all_gather(new_values, 'seq', axis=0, tiled=True)]
    all_gather x20 -> x0, blocking collectives: 365 us -> none  [the longest x5 101 us: run_block(): lax.all_gather(attended, 'head', axis=1, tiled=True)]
    pallas_call x0 -> x1, Pallas kernels: none -> 103 us  [per_device(): pl.pallas_call(functools.partial(block_kernel, nz, ny, nx, count, tok, he...]
    dot_general x20 -> x0, matrix products: 44.8 us -> none  [the longest x5 20.5 us: run_block(): jnp.dot(normed, weights_full, preferred_element_type=jnp.float32)]
    ppermute x5 -> x0, waiting for transfers between devices: 40.9 us -> none  [passed_along(): lax.ppermute(value, axis, [(source, source + steps) for source in range(l...]
    all_gather x11 -> x0, local copies, waits for them, and re-layouts: 25.8 us -> none  [the longest x1 10.2 us: per_device(): lax.all_gather(w_qkv[0], 'seq', axis=0, tiled=True)]
    another operation x1 -> x0, loops' own time: 20.7 us -> none  [per_device(): lax.fori_loop(0, patch_count + segment_count - 1, advance, initial_state)]
  transfers between devices with their start and end apart: 16 -> 0, of which waited for: 16 -> 0; matrix products, arithmetic and copies ran while one was open for 2% -> 0% of each run, Pallas kernels for 0% -> 0%
where the time goes in v1:
time: 114 us
  Pallas kernels  103 us (90%)
  local copies, waits for them, and re-layouts  9.98 us (9%)
    pallas_call x1, Pallas kernels, per_device(): pl.pallas_call(functools.partial(block_kernel, nz, ny, nx, count, tok, he...  103 us
    unnamed x21, local copies, waits for them, and re-layouts  9.98 us

profile of v1, /device:TPU:1, one launch (start us, length us, event | category | flops | bytes accessed | tf_op | source)
XLA Modules:
  0.0 113.6 jit_solution(9405300133150729782)
XLA Ops:
  0.6 0.0 copy-start
  0.6 1.7 %copy-done = bf16[1,3072,384]{2,1,0:T(8,128)(2,1)S(1)} copy-done((bf16[1,3072,384]{2,1,0:T(8,128)(2,1)S(1)}, bf16[1,3072,384]{2,1,0:T(8,128)(2,1)}, u32[]{:S(2)}) %copy-start) | copy-done | bytes 2359320
  2.3 0.0 copy-start.1
  2.3 1.0 copy-done.1
  3.3 0.0 copy-start.2
  3.3 0.9 copy-done.2
  4.2 0.0 copy-start.3
  4.2 0.9 copy-done.3
  5.1 0.0 copy-start.4
  5.1 0.9 copy-done.4
  6.0 0.0 copy-start.5
  6.0 0.8 copy-done.5
  6.7 0.0 copy-start.6
  6.7 0.7 copy-done.6
  7.4 0.0 copy-start.7
  7.4 0.7 copy-done.7
  8.1 0.0 copy-start.8
  8.1 0.7 copy-done.8
  8.7 103.0 %blocks.1 = (bf16[96,384]{1,0:T(8,128)(2,1)S(1)}, bf16[96,384]{1,0:T(8,128)(2,1)S(1)}, bf16[96,384]{1,0:T(8,128)(2,1)S(1)}) custom-call(s32[4]{0:T(128)S(1)} %copy-done.7, s32[4]{0:T(128)S(1)} %copy-done.8, bf16[96,384]{1,0:T(8,128)(2,1)S(1)} %bitcast.17, bf16[96,384]{1,0:T(8,128)(2,1)S(1)} %bitcast.18, bf16[96,384]{1,0:T(8,128)(2,1)S(1)} %bitcast.19, ...), custom_call_target="tpu_custom_call" | custom-call | tf_op jit(solution)/shard_map/blocks/pallas_call | solution.py:450
  111.7 0.6 copy.15
  112.4 0.6 copy.16
  113.0 0.6 copy.17
Async XLA Ops:
  0.6 1.7 %copy-start = (bf16[1,3072,384]{2,1,0:T(8,128)(2,1)S(1)}, bf16[1,3072,384]{2,1,0:T(8,128)(2,1)}, u32[]{:S(2)}) copy-start(bf16[1,3072,384]{2,1,0:T(8,128)(2,1)} %param.13) | copy-start | bytes 7077892
  2.3 1.0 copy-start.1
  3.3 0.9 copy-start.2
  4.2 0.9 copy-start.3
  5.1 0.9 copy-start.4
  6.0 0.8 copy-start.5
  6.7 0.7 copy-start.6
  7.4 0.7 copy-start.7
  8.1 0.7 copy-start.8

commit v2 on v1

--- a/solution.py
+++ b/solution.py
@@ -27,18 +27,22 @@
     patches,
     tok,
     head_dim,
-    order,
-    start,
+    order_h,
+    start_h,
     x_in,
     ck,
     cv,
     w,
     wo,
-    mod,
-    gain,
+    mod_h,
+    gain_h,
     bo,
     nk,
     nv,
+    order,
+    start,
+    mod,
+    gain,
     xg,
     ns,
     xe,
@@ -78,7 +82,6 @@
     r_s,
     r_r,
     hand_s,
-    hand_r,
     go,
 ):
     sec = lax.axis_index("section")
@@ -86,7 +89,7 @@
     seq = lax.axis_index("seq")
     y = seq // nx
     x = lax.rem(seq, nx)
-    rows, feat = x_in.shape
+    _, rows, feat = xg.shape
     chunk = ck.shape[0]
     heads = feat // head_dim
     width = nz * feat
@@ -106,6 +109,12 @@
         return (sec, z, y * nx + lax.rem(x + d, nx))
 
     other = (1 - sec, z, seq)
+
+    def next_block(d):
+        return (1, lax.rem(z + d, nz), seq)
+
+    def last_block(d):
+        return (0, lax.rem(z + d, nz), seq)
 
     def z_at(d):
         return lax.rem(z + d, nz)
@@ -133,7 +142,16 @@
     )
     for dev in partners:
         pl.semaphore_signal(barrier, inc=1, device_id=dev, device_id_type=MESH)
-    pl.semaphore_wait(barrier, len(partners))
+
+    @pl.when(sec == 1)
+    def _():
+        for d in range(1, nz):
+            pl.semaphore_signal(barrier, inc=1, device_id=last_block(d), device_id_type=MESH)
+        pl.semaphore_wait(barrier, len(partners))
+
+    @pl.when(sec == 0)
+    def _():
+        pl.semaphore_wait(barrier, len(partners) + nz - 1)
 
     my_w_rows = pl.ds(pl.multiple_of(x * w_rows, w_rows), w_rows)
     my_cache = pl.ds(pl.multiple_of(fresh + y * chunk, chunk), chunk)
@@ -142,10 +160,17 @@
         pltpu.make_async_copy(ck, kall.at[my_cache, :], loc.at[1]),
         pltpu.make_async_copy(cv, vall.at[my_cache, :], loc.at[2]),
         pltpu.make_async_copy(wo, wo_v, loc.at[3]),
-    ]
-
-    hand = copy(bo, xg.at[z], hand_s, hand_r, other)
-    z_copies = [copy(xg.at[z], xg.at[z], xg_s.at[d], xg_r.at[z], on_z(d)) for d in range(1, nz)]
+        pltpu.make_async_copy(order_h, order, loc.at[4]),
+        pltpu.make_async_copy(start_h, start, loc.at[5]),
+        pltpu.make_async_copy(mod_h, mod, loc.at[6]),
+        pltpu.make_async_copy(gain_h, gain, loc.at[7]),
+    ]
+    own_x = pltpu.make_async_copy(x_in, xg.at[z], loc.at[8])
+
+    z_copies = [copy(x_in, xg.at[z], xg_s.at[d], xg_r.at[z], on_z(d)) for d in range(1, nz)]
+    hand_copies = [
+        copy(bo, xg.at[z], hand_s.at[d], xg_r.at[z], next_block(d)) for d in range(nz)
+    ]
     w_copies = [
         copy(w, wbuf.at[:, my_w_rows, :], w_s.at[d], w_r.at[x], on_x(d)) for d in range(1, nx)
     ]
@@ -185,12 +210,11 @@
 
     @pl.when(sec == 0)
     def _():
-        xg[z] = x_in[...]
-        for c in z_copies + w_copies:
+        for c in z_copies + [own_x] + w_copies:
             c.start()
 
-    for c in local:
-        c.start()
+    for i in (4, 5, 6, 7, 0, 1, 2, 3):
+        local[i].start()
 
     @pl.when(sec == 1)
     def _():
@@ -201,6 +225,8 @@
         for c in cache_copies:
             c.start()
 
+    local[4].wait()
+    local[5].wait()
     places = [order[i] for i in range(patches)]
     begins = [start[i] for i in range(patches)]
     steps = [
@@ -230,11 +256,13 @@
         [jnp.where(lane == steps[p], 1.0, 0.0) for p in range(patches)], axis=0
     ).astype(BF16)
 
+    @pl.when(sec == 0)
+    def _():
+        own_x.wait()
+
     @pl.when(sec == 1)
     def _():
-        arrived(xg.at[z], hand_r)
-        for c in z_copies:
-            c.start()
+        arrived(xg.at[z], xg_r.at[z])
 
     for d in range(1, nz):
         arrived(xg.at[z_at(d)], xg_r.at[z_at(d)])
@@ -248,6 +276,8 @@
         total += diff * diff
     spread = jnp.sum(total, axis=-1, keepdims=True) * (1.0 / width)
     scale = lax.rsqrt(spread + 1e-06)
+    local[6].wait()
+    local[7].wait()
 
     def normed(i):
         at = pl.ds(pl.multiple_of(i * feat, feat), feat)
@@ -402,7 +432,8 @@
 
     @pl.when(sec == 0)
     def _():
-        hand.start()
+        for c in hand_copies:
+            c.start()
 
     for i in range(2):
         for d in range(1, nx):
@@ -421,12 +452,37 @@
 
     @pl.when(sec == 0)
     def _():
-        hand.wait_send()
-
-    for c in z_copies + w_copies + cache_copies + n_copies + q_copies + num_copies:
+        for c in z_copies + hand_copies:
+            c.wait_send()
+
+    for c in w_copies + cache_copies + n_copies + q_copies + num_copies:
         c.wait_send()
     for c in sum(p_copies, []) + sum(kv_copies, []) + a_copies + r_copies:
         c.wait_send()
+
+
+def write_kernel(*refs):
+    count = (len(refs) - 1) // 2
+    sem = refs[-1]
+    copies = [
+        pltpu.make_async_copy(refs[i], refs[count + i], sem.at[i]) for i in range(count)
+    ]
+    for c in copies:
+        c.start()
+    for c in copies:
+        c.wait()
+
+
+def written(*arrays):
+    return pl.pallas_call(
+        write_kernel,
+        name="write",
+        out_shape=tuple(jax.ShapeDtypeStruct(a.shape, a.dtype) for a in arrays),
+        in_specs=[pl.BlockSpec(memory_space=pl.ANY)] * len(arrays),
+        out_specs=(pl.BlockSpec(memory_space=pl.ANY),) * len(arrays),
+        scratch_shapes=[pltpu.SemaphoreType.DMA((len(arrays),))],
+        compiler_params=pltpu.CompilerParams(vmem_limit_bytes=60 << 20),
+    )(*arrays)
 
 
 def per_device(
@@ -445,7 +501,6 @@
     keys = ny * (rows + chunk)
     dma = pltpu.SemaphoreType.DMA
     vmem = pl.BlockSpec(memory_space=pltpu.VMEM)
-    smem = pl.BlockSpec(memory_space=pltpu.SMEM)
     hbm = pl.BlockSpec(memory_space=pl.ANY)
     out, new_k, new_v = pl.pallas_call(
         functools.partial(block_kernel, nz, ny, nx, count, tok, head_dim),
@@ -455,9 +510,13 @@
             jax.ShapeDtypeStruct((chunk, feat), BF16),
             jax.ShapeDtypeStruct((chunk, feat), BF16),
         ),
-        in_specs=[smem, smem, vmem, vmem, vmem, hbm, hbm, vmem, vmem],
+        in_specs=[hbm] * 9,
         out_specs=(vmem, vmem, vmem),
         scratch_shapes=[
+            pltpu.SMEM((count,), jnp.int32),
+            pltpu.SMEM((count,), jnp.int32),
+            pltpu.VMEM((3, 1, width), F32),
+            pltpu.VMEM((2, head_dim), F32),
             pltpu.VMEM((nz, rows, feat), BF16),
             pltpu.VMEM((ny, rows, hz * feat), BF16),
             pltpu.VMEM((ny, rows, hz * feat), BF16),
@@ -475,7 +534,7 @@
             pltpu.VMEM((nz, rows, feat), BF16),
             pltpu.VMEM((2, nx, pad, feat), BF16),
             pltpu.VMEM((2, nx, pad, feat), BF16),
-            dma((4,)),
+            dma((9,)),
             dma((nz,)),
             dma((nz,)),
             dma((ny,)),
@@ -496,12 +555,11 @@
             dma((nz,)),
             dma((2, nx)),
             dma((2, nx)),
-            dma,
-            dma,
+            dma((nz,)),
             pltpu.SemaphoreType.REGULAR((2,)),
         ],
         compiler_params=pltpu.CompilerParams(
-            collective_id=0, has_side_effects=True, vmem_limit_bytes=48 << 20
+            collective_id=0, has_side_effects=True, vmem_limit_bytes=60 << 20
         ),
     )(
         patch_order,
@@ -514,6 +572,7 @@
         jnp.transpose(modulation, (1, 0, 2)),
         qk_gain[0],
     )
+    out, new_k, new_v = written(out, new_k, new_v)
     return (out.reshape(1, count, tok, feat), new_k[None], new_v[None])
 
 

time: 114 us -> 112 us (0.982)
  local copies, waits for them, and re-layouts: 9.98 us -> 0 us
  Pallas kernels: 103 us -> 111 us
    unnamed x21 -> x0, local copies, waits for them, and re-layouts: 9.98 us -> none
    pallas_call x0 -> x1, Pallas kernels: none -> 7.83 us  [written(): pl.pallas_call(write_kernel, name='write', out_shape=tuple((jax.ShapeDtyp...]
where the time goes in v2:
time: 112 us
  Pallas kernels  111 us (99%)
    pallas_call x1, Pallas kernels, per_device(): pl.pallas_call(functools.partial(block_kernel, nz, ny, nx, count, tok, he...  103 us
    pallas_call x1, Pallas kernels, written(): pl.pallas_call(write_kernel, name='write', out_shape=tuple((jax.ShapeDtyp...  7.83 us

profile of v2, /device:TPU:1, one launch (start us, length us, event | category | flops | bytes accessed | tf_op | source)
XLA Modules:
  0.0 111.8 jit_solution(11821914915028611425)
XLA Ops:
  0.6 103.3 %blocks.1 = (bf16[96,384]{1,0:T(8,128)(2,1)}, bf16[96,384]{1,0:T(8,128)(2,1)}, bf16[96,384]{1,0:T(8,128)(2,1)}) custom-call(s32[4]{0:T(128)} %order_h.1, s32[4]{0:T(128)} %start_h.1, bf16[96,384]{1,0:T(8,128)(2,1)} %bitcast.14, bf16[96,384]{1,0:T(8,128)(2,1)} %bitcast.15, bf16[96,384]{1,0:T(8,128)(2,1)} %bitcast.16, bf16[3,192,384]{2,1,0:T(8,128)(2,1)} %bitcast.13, ...), custom_call_target="tpu_custom_call" | custom-call | tf_op jit(solution)/shard_map/blocks/pallas_call | solution.py:505
  103.9 7.8 %write.1 = (bf16[96,384]{1,0:T(8,128)(2,1)}, bf16[96,384]{1,0:T(8,128)(2,1)}, bf16[96,384]{1,0:T(8,128)(2,1)}) custom-call(bf16[96,384]{1,0:T(8,128)(2,1)} %get-tuple-element.9.refs_0_, bf16[96,384]{1,0:T(8,128)(2,1)} %get-tuple-element.10.refs_1_, bf16[96,384]{1,0:T(8,128)(2,1)} %get-tuple-element.11.refs_2_), custom_call_target="tpu_custom_call" | custom-call | tf_op jit(solution)/shard_map/write/pallas_call | solution.py:477

commit v3 on v2

v3 whole, which is shorter than its diff:
```python
import functools
import math

import jax
import jax.numpy as jnp
from jax import lax
from jax.experimental import pallas as pl
from jax.experimental.pallas import tpu as pltpu
from jax.sharding import PartitionSpec as P

MESH = pl.DeviceIdType.MESH
F32 = jnp.float32
BF16 = jnp.bfloat16
FAR = -1e30


def square_side(count):
    side = math.isqrt(count)
    assert side * side == count
    return side


def block_kernel(
    nz,
    ny,
    nx,
    patches,
    tok,
    head_dim,
    order_h,
    start_h,
    x_in,
    ck,
    cv,
    w,
    wo,
    mod_h,
    gain_h,
    bo,
    nk,
    nv,
    order,
    start,
    mod,
    gain,
    own,
    xr,
    xe,
    xg,
    xn,
    st_send,
    st_recv,
    st_norm,
    st_all,
    wbuf,
    wo_v,
    psend,
    precv,
    qg,
    kall,
    vall,
    bias,
    tag,
    nsend,
    nrecv,
    ag,
    rsend,
    rrecv,
    loc,
    x_s,
    x_r,
    st_s,
    st_r,
    sn_s,
    sn_r,
    h_s,
    h_r,
    w_s,
    w_r,
    wa_s,
    wa_r,
    wb_s,
    wb_r,
    wc_s,
    wc_r,
    wd_s,
    wd_r,
    c_s,
    c_r,
    p_s,
    p_r,
    q_s,
    q_r,
    kv_s,
    kv_r,
    n_s,
    n_r,
    ag_s,
    ag_r,
    r_s,
    r_r,
    go,
):
    sec = lax.axis_index("section")
    z = lax.axis_index("head")
    seq = lax.axis_index("seq")
    y = seq // nx
    x = lax.rem(seq, nx)
    rows, feat = own.shape
    chunk = ck.shape[0]
    heads = feat // head_dim
    width = nz * feat
    w_rows = w.shape[1]
    hz = nz // ny
    hy = z // hz
    fresh = ny * rows
    span = ny * chunk
    pad = rrecv.shape[2]

    def on_z(d):
        return (sec, lax.rem(z + d, nz), seq)

    def on_y(d):
        return (sec, z, lax.rem(y + d, ny) * nx + x)

    def on_x(d):
        return (sec, z, y * nx + lax.rem(x + d, nx))

    other = (1 - sec, z, seq)

    def z_at(d):
        return lax.rem(z + d, nz)

    def y_at(d):
        return lax.rem(y + d, ny)

    def x_at(d):
        return lax.rem(x + d, nx)

    def copy(src, dst, ss, rs, dev):
        return pltpu.make_async_remote_copy(
            src_ref=src, dst_ref=dst, send_sem=ss, recv_sem=rs, device_id=dev, device_id_type=MESH
        )

    def arrived(dst, rs):
        copy(dst, dst, rs, rs, other).wait_recv()

    w_slot = wbuf.at[:, y, x]
    my_cache = pl.ds(pl.multiple_of(fresh + y * chunk, chunk), chunk)
    own_x = pltpu.make_async_copy(x_in, own, loc.at[0])
    own_w = pltpu.make_async_copy(w, w_slot, loc.at[1])
    own_cache = [
        pltpu.make_async_copy(ck, kall.at[my_cache, :], loc.at[2]),
        pltpu.make_async_copy(cv, vall.at[my_cache, :], loc.at[3]),
    ]
    own_places = [
        pltpu.make_async_copy(order_h, order, loc.at[4]),
        pltpu.make_async_copy(start_h, start, loc.at[5]),
    ]
    own_scales = [
        pltpu.make_async_copy(mod_h, mod, loc.at[6]),
        pltpu.make_async_copy(gain_h, gain, loc.at[7]),
    ]
    own_wo = pltpu.make_async_copy(wo, wo_v, loc.at[8])

    slot = xr.at[y, lax.rem(z, hz)]
    slot_r = x_r.at[y, lax.rem(z, hz)]

    first_x = [
        copy(own, slot, x_s.at[d], slot_r, (0, z_at(d), hy * nx + x)) for d in range(nz)
    ]
    first_st = [
        copy(st_send, st_recv.at[z], st_s.at[d], st_r.at[z], on_z(d)) for d in range(1, nz)
    ]
    next_x = [
        copy(bo, xg.at[z], h_s.at[d], h_r.at[z], (1, z_at(d), seq)) for d in range(nz)
    ]
    sn_copies = [
        copy(st_norm, st_all.at[y], sn_s.at[d], sn_r.at[y], on_y(d)) for d in range(1, ny)
    ]
    w_copies = [copy(w_slot, w_slot, w_s.at[d], w_r.at[x], on_x(d)) for d in range(1, nx)]
    half = w_rows // 2
    upper, lower = pl.ds(0, half), pl.ds(half, half)

    def w_gather(view, ss, rs, at, to, count):
        return [copy(view, view, ss.at[d], rs.at[at], to(d)) for d in range(1, count)]

    wa_copies = w_gather(wbuf.at[:, y, x, upper], wa_s, wa_r, x, on_x, nx)
    wb_copies = w_gather(wbuf.at[:, y, x, lower], wb_s, wb_r, y, on_y, ny)
    wc_copies = [
        w_gather(wbuf.at[i, y, :, upper], wc_s.at[i], wc_r.at[i], y, on_y, ny) for i in range(3)
    ]
    wd_copies = [
        w_gather(wbuf.at[i, :, x, lower], wd_s.at[i], wd_r.at[i], x, on_x, nx) for i in range(3)
    ]
    cache_copies = [
        copy(ref.at[my_cache, :], ref.at[my_cache, :], c_s.at[i, d], c_r.at[i, y], on_y(d))
        for d in range(1, ny)
        for i, ref in enumerate((kall, vall))
    ]
    p_copies = [
        [
            copy(psend.at[i, y_at(d)], precv.at[i, y], p_s.at[i, d], p_r.at[i, y], on_y(d))
            for d in range(1, ny)
        ]
        for i in range(3)
    ]
    q_copies = [copy(qg.at[x], qg.at[x], q_s.at[d], q_r.at[x], on_x(d)) for d in range(1, nx)]
    my_fresh = pl.ds(pl.multiple_of(y * rows, rows), rows)
    kv_copies = [
        [
            copy(
                ref.at[my_fresh, :], ref.at[my_fresh, :], kv_s.at[i, d], kv_r.at[i, y], on_y(d)
            )
            for d in range(1, ny)
        ]
        for i, ref in enumerate((kall, vall))
    ]
    num_copies = [
        [
            copy(nsend.at[h, x_at(d)], nrecv.at[h, x], n_s.at[h, d], n_r.at[h, x], on_x(d))
            for d in range(1, nx)
        ]
        for h in range(heads)
    ]
    a_copies = [
        [
            copy(ag.at[h, z], ag.at[h, z], ag_s.at[h, d], ag_r.at[h, z], on_z(d))
            for d in range(1, nz)
        ]
        for h in range(heads)
    ]
    r_copies = [
        copy(rsend.at[i, x_at(d)], rrecv.at[i, x], r_s.at[i, d], r_r.at[i, x], on_x(d))
        for d in range(1, nx)
        for i in range(2)
    ]

    @pl.when(sec == 0)
    def _():
        own_x.start()

    for c in [own_w] + own_places + own_scales + own_cache + [own_wo]:
        c.start()

    barrier = pltpu.get_barrier_semaphore()

    def greet(dev):
        pl.semaphore_signal(barrier, inc=1, device_id=dev, device_id_type=MESH)

    partners = (
        [on_z(d) for d in range(1, nz)]
        + [on_y(d) for d in range(1, ny)]
        + [on_x(d) for d in range(1, nx)]
    )
    for dev in partners:
        greet(dev)

    def is_own(i, b):
        return (y == i) & (z == y * hz + b)

    @pl.when(sec == 0)
    def _():
        for i in range(ny):
            for b in range(hz):

                @pl.when(jnp.logical_not(is_own(i, b)))
                def _():
                    greet((0, y * hz + b, i * nx + x))

    @pl.when(sec == 1)
    def _():
        for d in range(nz):
            greet((0, z_at(d), seq))

    lane_rows = lax.broadcasted_iota(jnp.int32, (rows, head_dim), 1)

    def shard_stats(value):
        value = value.astype(F32)
        middle = jnp.sum(value, axis=-1, keepdims=True) * (1.0 / feat)
        value = value - middle
        square = jnp.sum(value * value, axis=-1, keepdims=True)
        both = jnp.where(lane_rows == 0, middle, jnp.where(lane_rows == 1, square, 0.0))
        both = jnp.concatenate([both, jnp.zeros((head_dim - rows, head_dim), F32)], axis=0)
        st_send[...] = jnp.transpose(both)[0:8, :]

    @pl.when(sec == 0)
    def _():
        own_x.wait()
        shard_stats(own[...])
        st_recv[z] = st_send[...]
        pl.semaphore_wait(barrier, len(partners) + 2 * nz - jnp.where(hy == y, 1, 0))
        for c in first_st + first_x[1:]:
            c.start()

        @pl.when(hy == y)
        def _():
            slot[...] = own[...]

        @pl.when(hy != y)
        def _():
            first_x[0].start()

    own_w.wait()
    for c in own_cache:
        c.wait()

    @pl.when(sec == 0)
    def _():
        for c in w_copies + cache_copies:
            c.start()

    @pl.when(sec == 1)
    def _():
        pl.semaphore_wait(barrier, len(partners))
        for c in wb_copies:
            c.start()
        pl.semaphore_wait(go.at[0], 1)
        for c in wa_copies:
            c.start()
        for d in range(1, ny):
            arrived(wbuf.at[:, y_at(d), x, lower], wb_r.at[y_at(d)])
        for d in range(1, nx):
            arrived(wbuf.at[:, y, x_at(d), upper], wa_r.at[x_at(d)])
        for c in wd_copies[1] + wd_copies[0]:
            c.start()
        pl.semaphore_wait(go.at[1], 1)
        for c in wc_copies[1] + wc_copies[0] + cache_copies + wc_copies[2]:
            c.start()
        pl.semaphore_wait(go.at[2], 1)
        for c in wd_copies[2]:
            c.start()

    for c in own_places:
        c.wait()
    places = [order[i] for i in range(patches)]
    begins = [start[i] for i in range(patches)]
    steps = [
        sum(jnp.where(places[s] == p, s, 0) for s in range(patches)) for p in range(patches)
    ]

    def first_after(step, pos):
        found = patches
        for p in range(patches):
            hit = (steps[p] > step) & (begins[p] <= pos) & (pos < begins[p] + span)
            found = jnp.where(hit, jnp.minimum(found, steps[p]), found)
        return found

    lane = lax.broadcasted_iota(jnp.int32, (tok, head_dim), 1)
    lane_chunk = lax.broadcasted_iota(jnp.int32, (chunk, head_dim), 1)
    for j in range(ny):
        parts = []
        for p in range(patches):
            upto = first_after(steps[p], begins[p] + j * chunk)
            parts.append(jnp.where((lane >= steps[p]) & (lane < upto), 0.0, FAR))
        bias[j * rows : (j + 1) * rows, :] = jnp.concatenate(parts, axis=0).astype(BF16)
        upto = first_after(-1, (j * nx + x) * chunk)
        bias[fresh + j * chunk : fresh + (j + 1) * chunk, :] = jnp.where(
            lane_chunk < upto, 0.0, FAR
        ).astype(BF16)
    tag[...] = jnp.concatenate(
        [jnp.where(lane == steps[p], 1.0, 0.0) for p in range(patches)], axis=0
    ).astype(BF16)

    for c in own_scales:
        c.wait()

    def rms_heads(value, which):
        out = []
        for h in range(heads):
            part = value[:, h * head_dim : (h + 1) * head_dim]
            power = jnp.sum(part * part, axis=-1, keepdims=True) * (1.0 / head_dim)
            out.append(part * lax.rsqrt(power + 1e-06) * gain[which : which + 1, :])
        return jnp.concatenate(out, axis=-1).astype(BF16)

    def spread_part(i, value):
        if i == 0:
            qg[x] = rms_heads(value, 0)
            copies = q_copies
        elif i == 1:
            kall[my_fresh, :] = rms_heads(value, 1)
            copies = kv_copies[0]
        else:
            vall[my_fresh, :] = value.astype(BF16)
            copies = kv_copies[1]
        for c in copies:
            c.start()

    @pl.when(sec == 0)
    def _():
        for d in range(1, nz):
            arrived(st_recv.at[z_at(d)], st_r.at[z_at(d)])
        middles = [st_recv[i, 0:1, :] for i in range(nz)]
        mean = sum(middles) * (1.0 / nz)
        square = sum(st_recv[i, 1:2, :] for i in range(nz))
        square += sum((m - mean) * (m - mean) for m in middles) * feat
        scale = lax.rsqrt(square * (1.0 / width) + 1e-06)
        line = lax.broadcasted_iota(jnp.int32, (8, head_dim), 0)
        value = jnp.where(line == 0, mean, jnp.where(line == 1, scale, 0.0))
        st_norm[...] = value
        st_all[y] = value
        for c in sn_copies:
            c.start()
        for d in range(1, ny):
            arrived(st_all.at[y_at(d)], sn_r.at[y_at(d)])
        value = st_all[...].reshape(8 * ny, head_dim)
        value = jnp.concatenate([value, jnp.zeros((head_dim - 8 * ny, head_dim), F32)], axis=0)
        stats = jnp.transpose(value)[0:rows, :]
        for d in range(1, nx):
            arrived(wbuf.at[:, y, x_at(d)], w_r.at[x_at(d)])
        pl.semaphore_signal(go.at[0], inc=1, device_id=other, device_id_type=MESH)
        for i in range(ny):
            for b in range(hz):

                @pl.when(jnp.logical_not(is_own(i, b)))
                def _():
                    arrived(xr.at[i, b], x_r.at[i, b])

                at = pl.ds(pl.multiple_of((y * hz + b) * feat, feat), feat)
                value = xr[i, b].astype(F32) - stats[:, 8 * i : 8 * i + 1]
                value = value * stats[:, 8 * i + 1 : 8 * i + 2]
                value = value * (1.0 + mod[1, :, at]) + mod[0, :, at]
                xe[i, :, b * feat : (b + 1) * feat] = value.astype(BF16)

        tokens = xe[...].reshape(ny * rows, hz * feat)
        for i in (1, 0, 2):
            weights = wbuf[i, y].reshape(nx * w_rows, feat)
            value = jnp.dot(tokens, weights, preferred_element_type=F32)
            psend[i] = value.astype(BF16).reshape(ny, rows, feat)
            for c in p_copies[i]:
                c.start()
        for i in (1, 0, 2):
            value = psend[i, y].astype(F32)
            for d in range(1, ny):
                arrived(precv.at[i, y_at(d)], p_r.at[i, y_at(d)])
                value += precv[i, y_at(d)].astype(F32)
            spread_part(i, value)

    @pl.when(sec == 1)
    def _():
        for i in range(nz):
            arrived(xg.at[i], h_r.at[i])
        own[...] = xg[z]
        total = jnp.zeros((rows, feat), F32)
        for i in range(nz):
            total += xg[i].astype(F32)
        mean = jnp.sum(total, axis=-1, keepdims=True) * (1.0 / width)
        total = jnp.zeros((rows, feat), F32)
        for i in range(nz):
            diff = xg[i].astype(F32) - mean
            total += diff * diff
        scale = lax.rsqrt(jnp.sum(total, axis=-1, keepdims=True) * (1.0 / width) + 1e-06)
        for i in range(nz):
            at = slice(i * feat, (i + 1) * feat)
            value = (xg[i].astype(F32) - mean) * scale * (1.0 + mod[1, :, at]) + mod[0, :, at]
            xn[:, at] = value.astype(BF16)
        for i in (1, 0, 2):
            for d in range(1, ny):
                arrived(wbuf.at[i, y_at(d), :, upper], wc_r.at[i, y_at(d)])
            for d in range(1, nx):
                arrived(wbuf.at[i, :, x_at(d), lower], wd_r.at[i, x_at(d)])
            weights = wbuf[i].reshape(width, feat)
            spread_part(i, jnp.dot(xn[...], weights, preferred_element_type=F32))

    for i, ref in enumerate((kall, vall)):
        for d in range(1, ny):
            at = pl.ds(pl.multiple_of(fresh + y_at(d) * chunk, chunk), chunk)
            arrived(ref.at[at, :], c_r.at[i, y_at(d)])
    for i, ref in enumerate((kall, vall)):
        for d in range(1, ny):
            at = pl.ds(pl.multiple_of(y_at(d) * rows, rows), rows)
            arrived(ref.at[at, :], kv_r.at[i, y_at(d)])
    for d in range(1, nx):
        arrived(qg.at[x_at(d)], q_r.at[x_at(d)])

    @pl.when(sec == 0)
    def _():
        pl.semaphore_signal(go.at[1], inc=1, device_id=other, device_id_type=MESH)

    tags = jnp.concatenate([tag[...]] * nx, axis=0)
    lane_all = lax.broadcasted_iota(jnp.int32, (nx * rows, head_dim), 1)
    exponent = math.log2(math.e) / math.sqrt(head_dim)
    for h in range(heads):
        at = slice(h * head_dim, (h + 1) * head_dim)
        queries = jnp.concatenate([qg[:, :, at].reshape(nx * rows, head_dim), tags], axis=1)
        keys = jnp.concatenate([kall[:, at], bias[...]], axis=1)
        scores = lax.dot_general(
            queries, keys, (((1,), (1,)), ((), ())), preferred_element_type=F32
        )
        weight = jnp.exp2(scores * exponent)
        denom = jnp.sum(weight, axis=-1, keepdims=True)
        numer = jnp.dot(weight.astype(BF16), vall[:, at], preferred_element_type=F32)
        nsend[h, :, :, 0:head_dim] = numer.astype(BF16).reshape(nx, rows, head_dim)
        high = denom.astype(BF16).astype(F32)
        sums = jnp.where(lane_all == 0, high, denom - high)
        nsend[h, :, :, head_dim:] = sums.astype(BF16).reshape(nx, rows, head_dim)
        for c in num_copies[h]:
            c.start()

    for h in range(heads):
        total = nsend[h, x].astype(F32)
        for d in range(1, nx):
            arrived(nrecv.at[h, x_at(d)], n_r.at[h, x_at(d)])
            total += nrecv[h, x_at(d)].astype(F32)
        denom = total[:, head_dim : head_dim + 1] + total[:, head_dim + 1 : head_dim + 2]
        ag[h, z] = (total[:, 0:head_dim] / denom).astype(BF16)
        for c in a_copies[h]:
            c.start()

    @pl.when(sec == 0)
    def _():
        pl.semaphore_signal(go.at[2], inc=1, device_id=other, device_id_type=MESH)

    def source(c):
        pos = c * chunk
        last = -1
        first_row = -fresh - pad
        for p in range(patches):
            hit = (begins[p] <= pos) & (pos < begins[p] + span) & (steps[p] > last)
            last = jnp.where(hit, steps[p], last)
            row = (pos - begins[p]) // chunk * rows + p * tok
            first_row = jnp.where(hit, row, first_row)
        return first_row, last

    in_row = lax.broadcasted_iota(jnp.int32, (pad, fresh), 0)
    in_col = lax.broadcasted_iota(jnp.int32, (pad, fresh), 1)
    picks = []
    for c in range(nx):
        first_row, _ = source(y * nx + c)
        hit = (in_col - in_row == first_row) & (in_row < tok)
        picks.append(jnp.where(hit, 1.0, 0.0).astype(BF16))
    pick = jnp.concatenate(picks, axis=0)
    for i, ref in enumerate((kall, vall)):
        value = jnp.dot(pick, ref[0:fresh, :], preferred_element_type=F32)
        rsend[i] = value.astype(BF16).reshape(nx, pad, feat)
    for c in r_copies:
        c.start()

    own_wo.wait()
    result = jnp.zeros((rows, feat), F32)
    for h in range(heads):
        for d in range(1, nz):
            arrived(ag.at[h, z_at(d)], ag_r.at[h, z_at(d)])
        attended = jnp.concatenate([ag[h, i] for i in range(nz)], axis=1)
        weights = wo_v[:, h].reshape(nz * head_dim, feat)
        result += jnp.dot(attended, weights, preferred_element_type=F32)
    gate = mod[2, :, pl.ds(pl.multiple_of(z * feat, feat), feat)]
    bo[...] = (own[...].astype(F32) + gate * result).astype(BF16)

    @pl.when(sec == 0)
    def _():
        for c in next_x:
            c.start()

    for i in range(2):
        for d in range(1, nx):
            arrived(rrecv.at[i, x_at(d)], r_r.at[i, x_at(d)])
        rrecv[i, x] = rsend[i, x]
    out_row = lax.broadcasted_iota(jnp.int32, (chunk, nx * pad), 0)
    out_col = lax.broadcasted_iota(jnp.int32, (chunk, nx * pad), 1)
    block = out_col // pad
    within = out_col - block * pad
    hit = (out_row == block * tok + within) & (within < tok)
    place = jnp.where(hit, 1.0, 0.0).astype(BF16)
    _, last = source(seq)
    for i, (old, new) in enumerate(((kall, nk), (vall, nv))):
        value = jnp.dot(place, rrecv[i].reshape(nx * pad, feat), preferred_element_type=F32)
        new[...] = jnp.where(last >= 0, value, old[my_cache, :].astype(F32)).astype(BF16)

    @pl.when(sec == 0)
    def _():
        for c in next_x + first_st + first_x[1:] + sn_copies + w_copies + sum(p_copies, []):
            c.wait_send()

        @pl.when(hy != y)
        def _():
            first_x[0].wait_send()

    @pl.when(sec == 1)
    def _():
        for c in wa_copies + wb_copies + sum(wc_copies + wd_copies, []):
            c.wait_send()

    for c in cache_copies + q_copies + r_copies + sum(kv_copies + num_copies + a_copies, []):
        c.wait_send()


def write_kernel(*refs):
    half = len(refs) // 2
    for src, dst in zip(refs[:half], refs[half:]):
        dst[...] = src[...]


def written(*arrays):
    vmem = pl.BlockSpec(memory_space=pltpu.VMEM)
    return pl.pallas_call(
        write_kernel,
        name="write",
        out_shape=tuple(jax.ShapeDtypeStruct(a.shape, a.dtype) for a in arrays),
        in_specs=[vmem] * len(arrays),
        out_specs=(vmem,) * len(arrays),
        compiler_params=pltpu.CompilerParams(vmem_limit_bytes=60 << 20),
    )(*arrays)


def per_device(
    patches, cache_k, cache_v, w_qkv, w_out, modulation, qk_gain, patch_order, patch_start
):
    nz = lax.axis_size("head")
    ny = nx = square_side(lax.axis_size("seq"))
    count, tok, feat = patches.shape
    chunk = cache_k.shape[1]
    head_dim = qk_gain.shape[-1]
    rows = count * tok
    hz = nz // ny
    heads = feat // head_dim
    w_rows = w_qkv.shape[1]
    pad = -(-tok // 16) * 16
    keys = ny * (rows + chunk)
    dma = pltpu.SemaphoreType.DMA
    vmem = pl.BlockSpec(memory_space=pltpu.VMEM)
    hbm = pl.BlockSpec(memory_space=pl.ANY)
    out, new_k, new_v = pl.pallas_call(
        functools.partial(block_kernel, nz, ny, nx, count, tok, head_dim),
        name="blocks",
        out_shape=(
            jax.ShapeDtypeStruct((rows, feat), BF16),
            jax.ShapeDtypeStruct((chunk, feat), BF16),
            jax.ShapeDtypeStruct((chunk, feat), BF16),
        ),
        in_specs=[hbm] * 9,
        out_specs=(vmem, vmem, vmem),
        scratch_shapes=[
            pltpu.SMEM((count,), jnp.int32),
            pltpu.SMEM((count,), jnp.int32),
            pltpu.VMEM((3, 1, nz * feat), F32),
            pltpu.VMEM((2, head_dim), F32),
            pltpu.VMEM((rows, feat), BF16),
            pltpu.VMEM((ny, hz, rows, feat), BF16),
            pltpu.VMEM((ny, rows, hz * feat), BF16),
            pltpu.VMEM((nz, rows, feat), BF16),
            pltpu.VMEM((rows, nz * feat), BF16),
            pltpu.VMEM((8, head_dim), F32),
            pltpu.VMEM((nz, 8, head_dim), F32),
            pltpu.VMEM((8, head_dim), F32),
            pltpu.VMEM((ny, 8, head_dim), F32),
            pltpu.VMEM((3, ny, nx, w_rows, feat), BF16),
            pltpu.VMEM((nz, heads, head_dim, feat), BF16),
            pltpu.VMEM((3, ny, rows, feat), BF16),
            pltpu.VMEM((3, ny, rows, feat), BF16),
            pltpu.VMEM((nx, rows, feat), BF16),
            pltpu.VMEM((keys, feat), BF16),
            pltpu.VMEM((keys, feat), BF16),
            pltpu.VMEM((keys, head_dim), BF16),
            pltpu.VMEM((rows, head_dim), BF16),
            pltpu.VMEM((heads, nx, rows, 2 * head_dim), BF16),
            pltpu.VMEM((heads, nx, rows, 2 * head_dim), BF16),
            pltpu.VMEM((heads, nz, rows, head_dim), BF16),
            pltpu.VMEM((2, nx, pad, feat), BF16),
            pltpu.VMEM((2, nx, pad, feat), BF16),
            dma((9,)),
            dma((nz,)),
            dma((ny, hz)),
            dma((nz,)),
            dma((nz,)),
            dma((ny,)),
            dma((ny,)),
            dma((nz,)),
            dma((nz,)),
            dma((nx,)),
            dma((nx,)),
            dma((nx,)),
            dma((nx,)),
            dma((ny,)),
            dma((ny,)),
            dma((3, ny)),
            dma((3, ny)),
            dma((3, nx)),
            dma((3, nx)),
            dma((2, ny)),
            dma((2, ny)),
            dma((3, ny)),
            dma((3, ny)),
            dma((nx,)),
            dma((nx,)),
            dma((2, ny)),
            dma((2, ny)),
            dma((heads, nx)),
            dma((heads, nx)),
            dma((heads, nz)),
            dma((heads, nz)),
            dma((2, nx)),
            dma((2, nx)),
            pltpu.SemaphoreType.REGULAR((3,)),
        ],
        compiler_params=pltpu.CompilerParams(
            collective_id=0, has_side_effects=True, vmem_limit_bytes=60 << 20
        ),
    )(
        patch_order,
        patch_start,
        patches.reshape(rows, feat),
        cache_k[0],
        cache_v[0],
        jnp.transpose(w_qkv[0], (1, 0, 2)),
        w_out[0].reshape(nz, feat // head_dim, head_dim, feat),
        jnp.transpose(modulation, (1, 0, 2)),
        qk_gain[0],
    )
    out, new_k, new_v = written(out, new_k, new_v)
    return (out.reshape(1, count, tok, feat), new_k[None], new_v[None])


def solution(mesh):
    return jax.shard_map(
        per_device,
        mesh=mesh,
        in_specs=(
            P(None, "seq", "head"),
            P("section", "seq", "head"),
            P("section", "seq", "head"),
            P("section", "seq", None, "head"),
            P("section", None, "head"),
            P("section", None, None),
            P("section", None, None),
            P(),
            P(),
        ),
        out_specs=(
            P("section", None, "seq", "head"),
            P("section", "seq", "head"),
            P("section", "seq", "head"),
        ),
        check_vma=False,
    )
```

time: 112 us -> 94 us (0.84)
  Pallas kernels: 111 us -> 93.2 us
    pallas_call x1, Pallas kernels: 103 us -> 91.6 us  [per_device(): pl.pallas_call(functools.partial(block_kernel, nz, ny, nx, count, tok, he...]
    pallas_call x1, Pallas kernels: 7.83 us -> 1.65 us  [written(): pl.pallas_call(write_kernel, name='write', out_shape=tuple((jax.ShapeDtyp...]
where the time goes in v3:
time: 94 us; the launch traced here: 93.9 us
  Pallas kernels  93.2 us (99%)
    pallas_call x1, Pallas kernels, per_device(): pl.pallas_call(functools.partial(block_kernel, nz, ny, nx, count, tok, he...  91.6 us

profile of v3, /device:TPU:1, one launch (start us, length us, event | category | flops | bytes accessed | tf_op | source)
XLA Modules:
  0.0 93.9 jit_solution(252844337987866126)
XLA Ops:
  0.6 91.6 %blocks.1 = (bf16[96,384]{1,0:T(8,128)(2,1)}, bf16[96,384]{1,0:T(8,128)(2,1)}, bf16[96,384]{1,0:T(8,128)(2,1)}) custom-call(s32[4]{0:T(128)} %order_h.1, s32[4]{0:T(128)} %start_h.1, bf16[96,384]{1,0:T(8,128)(2,1)} %bitcast.14, bf16[96,384]{1,0:T(8,128)(2,1)} %bitcast.15, bf16[96,384]{1,0:T(8,128)(2,1)} %bitcast.16, bf16[3,192,384]{2,1,0:T(8,128)(2,1)} %bitcast.13, ...), custom_call_target="tpu_custom_call" | custom-call | tf_op jit(solution)/shard_map/blocks/pallas_call | solution.py:623
  92.2 1.6 %write.1 = (bf16[96,384]{1,0:T(8,128)(2,1)}, bf16[96,384]{1,0:T(8,128)(2,1)}, bf16[96,384]{1,0:T(8,128)(2,1)}) custom-call(bf16[96,384]{1,0:T(8,128)(2,1)} %get-tuple-element.9.refs_0_, bf16[96,384]{1,0:T(8,128)(2,1)} %get-tuple-element.10.refs_1_, bf16[96,384]{1,0:T(8,128)(2,1)} %get-tuple-element.11.refs_2_), custom_call_target="tpu_custom_call" | custom-call | tf_op jit(solution)/shard_map/write/pallas_call | solution.py:596

commit v4 on v3

v4 whole, which is shorter than its diff:
```python
import functools
import math

import jax
import jax.numpy as jnp
from jax import lax
from jax.experimental import pallas as pl
from jax.experimental.pallas import tpu as pltpu
from jax.sharding import PartitionSpec as P

MESH = pl.DeviceIdType.MESH
F32 = jnp.float32
BF16 = jnp.bfloat16
FAR = -1e30


def square_side(count):
    side = math.isqrt(count)
    assert side * side == count
    return side


def block_kernel(
    nz,
    ny,
    nx,
    tok,
    waves,
    per_wave,
    head_dim,
    order_h,
    start_h,
    x_in,
    ck,
    cv,
    w,
    wo,
    mod_h,
    gain_h,
    bo,
    nk,
    nv,
    order,
    start,
    mod,
    gain,
    x_rows,
    own,
    done,
    xr,
    xe,
    xg,
    xn,
    st_send,
    st_recv,
    st_norm,
    st_all,
    wbuf,
    wo_v,
    psend,
    precv,
    qg,
    kv,
    bias,
    nsend,
    nrecv,
    ag,
    rsend,
    rrecv,
    loc,
    x_s,
    x_r,
    st_s,
    st_r,
    sn_s,
    sn_r,
    h_s,
    h_r,
    w_s,
    w_r,
    wa_s,
    wa_r,
    wb_s,
    wb_r,
    wc_s,
    wc_r,
    wd_s,
    wd_r,
    c_s,
    c_r,
    p_s,
    p_r,
    q_s,
    q_r,
    kv_s,
    kv_r,
    n_s,
    n_r,
    ag_s,
    ag_r,
    r_s,
    r_r,
    go,
):
    sec = lax.axis_index("section")
    z = lax.axis_index("head")
    seq = lax.axis_index("seq")
    y = seq // nx
    x = lax.rem(seq, nx)
    _, rows, feat = own.shape
    chunk = ck.shape[0]
    heads = feat // head_dim
    width = nz * feat
    w_rows = w.shape[1]
    hz = nz // ny
    hy = z // hz
    steps = waves * per_wave
    stale = ny * chunk
    fresh = ny * rows
    span = ny * chunk
    pad = rrecv.shape[1]

    def z_at(d):
        return lax.rem(z + d, nz)

    def y_at(d):
        return lax.rem(y + d, ny)

    def x_at(d):
        return lax.rem(x + d, nx)

    def on_z(d):
        return (sec, z_at(d), seq)

    def on_y(d):
        return (sec, z, y_at(d) * nx + x)

    def on_x(d):
        return (sec, z, y * nx + x_at(d))

    other = (1 - sec, z, seq)

    def copy(src, dst, ss, rs, dev):
        return pltpu.make_async_remote_copy(
            src_ref=src, dst_ref=dst, send_sem=ss, recv_sem=rs, device_id=dev, device_id_type=MESH
        )

    def arrived(dst, rs):
        copy(dst, dst, rs, rs, other).wait_recv()

    def cached(i):
        return pl.ds(pl.multiple_of(i * chunk, chunk), chunk)

    def freshly(v, i):
        return pl.ds(pl.multiple_of(stale + v * fresh + i * rows, rows), rows)

    w_slot = wbuf.at[:, y, x]
    own_x = pltpu.make_async_copy(x_in, x_rows, loc.at[0])
    own_w = pltpu.make_async_copy(w, w_slot, loc.at[1])
    own_cache = [
        pltpu.make_async_copy(ck, kv.at[cached(y), 0:feat], loc.at[2]),
        pltpu.make_async_copy(cv, kv.at[cached(y), feat : 2 * feat], loc.at[3]),
    ]
    own_places = [
        pltpu.make_async_copy(order_h, order, loc.at[4]),
        pltpu.make_async_copy(start_h, start, loc.at[5]),
    ]
    own_scales = [
        pltpu.make_async_copy(mod_h, mod, loc.at[6]),
        pltpu.make_async_copy(gain_h, gain, loc.at[7]),
    ]
    own_wo = pltpu.make_async_copy(wo, wo_v, loc.at[8])

    def by_wave(make):
        return [make(v) for v in range(waves)]

    first_x = by_wave(
        lambda v: [
            copy(
                own.at[v],
                xr.at[v, y, lax.rem(z, hz)],
                x_s.at[v, d],
                x_r.at[v, y, lax.rem(z, hz)],
                (0, z_at(d), hy * nx + x),
            )
            for d in range(nz)
        ]
    )
    first_st = [
        copy(st_send, st_recv.at[z], st_s.at[d], st_r.at[z], on_z(d)) for d in range(1, nz)
    ]
    next_x = by_wave(
        lambda v: [
            copy(done.at[v], xg.at[v, z], h_s.at[v, d], h_r.at[v, z], (1, z_at(d), seq))
            for d in range(nz)
        ]
    )
    sn_copies = [
        copy(st_norm, st_all.at[y], sn_s.at[d], sn_r.at[y], on_y(d)) for d in range(1, ny)
    ]
    w_copies = [copy(w_slot, w_slot, w_s.at[d], w_r.at[x], on_x(d)) for d in range(1, nx)]
    half = w_rows // 2
    upper, lower = pl.ds(0, half), pl.ds(half, half)

    def w_gather(view, ss, rs, at, to, count):
        return [copy(view, view, ss.at[d], rs.at[at], to(d)) for d in range(1, count)]

    wa_copies = w_gather(wbuf.at[:, y, x, upper], wa_s, wa_r, x, on_x, nx)
    wb_copies = w_gather(wbuf.at[:, y, x, lower], wb_s, wb_r, y, on_y, ny)
    wc_copies = [
        w_gather(wbuf.at[i, y, :, upper], wc_s.at[i], wc_r.at[i], y, on_y, ny) for i in range(3)
    ]
    wd_copies = [
        w_gather(wbuf.at[i, :, x, lower], wd_s.at[i], wd_r.at[i], x, on_x, nx) for i in range(3)
    ]
    cache_slot = kv.at[cached(y), :]
    cache_copies = [copy(cache_slot, cache_slot, c_s.at[d], c_r.at[y], on_y(d)) for d in range(1, ny)]
    p_copies = by_wave(
        lambda v: [
            copy(psend.at[v, y_at(d)], precv.at[v, y], p_s.at[v, d], p_r.at[v, y], on_y(d))
            for d in range(1, ny)
        ]
    )
    q_copies = by_wave(
        lambda v: [
            copy(qg.at[v, x], qg.at[v, x], q_s.at[v, d], q_r.at[v, x], on_x(d))
            for d in range(1, nx)
        ]
    )
    kv_copies = by_wave(
        lambda v: [
            copy(
                kv.at[freshly(v, y), :],
                kv.at[freshly(v, y), :],
                kv_s.at[v, d],
                kv_r.at[v, y],
                on_y(d),
            )
            for d in range(1, ny)
        ]
    )
    num_copies = by_wave(
        lambda v: [
            copy(nsend.at[v, x_at(d)], nrecv.at[v, x], n_s.at[v, d], n_r.at[v, x], on_x(d))
            for d in range(1, nx)
        ]
    )
    a_copies = by_wave(
        lambda v: [
            copy(ag.at[v, z], ag.at[v, z], ag_s.at[v, d], ag_r.at[v, z], on_z(d))
            for d in range(1, nz)
        ]
    )
    r_copies = [
        copy(rsend.at[x_at(d)], rrecv.at[x], r_s.at[d], r_r.at[x], on_x(d)) for d in range(1, nx)
    ]

    @pl.when(sec == 0)
    def _():
        own_x.start()

    for c in own_places + [own_w] + own_cache + own_scales + [own_wo]:
        c.start()

    barrier = pltpu.get_barrier_semaphore()

    def greet(dev):
        pl.semaphore_signal(barrier, inc=1, device_id=dev, device_id_type=MESH)

    partners = (
        [on_z(d) for d in range(1, nz)]
        + [on_y(d) for d in range(1, ny)]
        + [on_x(d) for d in range(1, nx)]
    )
    for dev in partners:
        greet(dev)

    def is_own(i, b):
        return (y == i) & (z == y * hz + b)

    @pl.when(sec == 0)
    def _():
        for i in range(ny):
            for b in range(hz):

                @pl.when(jnp.logical_not(is_own(i, b)))
                def _():
                    greet((0, y * hz + b, i * nx + x))

    @pl.when(sec == 1)
    def _():
        for d in range(nz):
            greet((0, z_at(d), seq))

    for c in own_places:
        c.wait()
    places = [order[s] for s in range(steps)]
    begins = [sum(jnp.where(places[s] == p, start[p], 0) for p in range(steps)) for s in range(steps)]

    lane_rows = lax.broadcasted_iota(jnp.int32, (steps * tok, head_dim), 1)

    def shard_stats(value):
        middle = jnp.sum(value, axis=-1, keepdims=True) * (1.0 / feat)
        value = value - middle
        square = jnp.sum(value * value, axis=-1, keepdims=True)
        both = jnp.where(lane_rows == 0, middle, jnp.where(lane_rows == 1, square, 0.0))
        both = jnp.concatenate([both, jnp.zeros((head_dim - steps * tok, head_dim), F32)], axis=0)
        st_send[...] = jnp.transpose(both)[0:8, :]

    @pl.when(sec == 0)
    def _():
        own_x.wait()
        value = x_rows[...].astype(F32)
        parts = [value[p * tok : (p + 1) * tok] for p in range(steps)]
        value = []
        for s in range(steps):
            chosen = parts[0]
            for p in range(1, steps):
                chosen = jnp.where(places[s] == p, parts[p], chosen)
            value.append(chosen)
        value = jnp.concatenate(value, axis=0)
        own[...] = value.astype(BF16).reshape(waves, rows, feat)
        shard_stats(value)
        st_recv[z] = st_send[...]
        pl.semaphore_wait(barrier, len(partners) + 2 * nz - jnp.where(hy == y, 1, 0))
        for c in first_st:
            c.start()
        for v in range(waves):
            for c in first_x[v][1:]:
                c.start()

            @pl.when(hy == y)
            def _():
                xr[v, y, lax.rem(z, hz)] = own[v]

            @pl.when(hy != y)
            def _():
                first_x[v][0].start()

    own_w.wait()
    for c in own_cache:
        c.wait()

    @pl.when(sec == 0)
    def _():
        for c in w_copies + cache_copies:
            c.start()

    @pl.when(sec == 1)
    def _():
        pl.semaphore_wait(barrier, len(partners))
        for c in wb_copies:
            c.start()
        pl.semaphore_wait(go.at[0], 1)
        for c in wa_copies:
            c.start()
        for d in range(1, ny):
            arrived(wbuf.at[:, y_at(d), x, lower], wb_r.at[y_at(d)])
        for c in wd_copies[1]:
            c.start()
        for d in range(1, nx):
            arrived(wbuf.at[:, y, x_at(d), upper], wa_r.at[x_at(d)])
        for c in wd_copies[0]:
            c.start()
        pl.semaphore_wait(go.at[1], 1)
        for c in wc_copies[1] + wc_copies[0] + wc_copies[2] + wd_copies[2] + cache_copies:
            c.start()
        pl.semaphore_wait(go.at[2], 1)

    def covers(s, pos):
        return (begins[s] <= pos) & (pos < begins[s] + span)

    def first_from(step, pos):
        found = steps
        for s in reversed(range(step, steps)):
            found = jnp.where(covers(s, pos), s, found)
        return found

    lane = lax.broadcasted_iota(jnp.int32, (tok, head_dim), 1)
    lane_chunk = lax.broadcasted_iota(jnp.int32, (chunk, head_dim), 1)
    for j in range(ny):
        upto = first_from(0, (j * nx + x) * chunk)
        value = jnp.where(lane_chunk < upto, 0.0, FAR)
        bias[j * chunk : (j + 1) * chunk, :] = value.astype(BF16)
        for v in range(waves):
            parts = []
            for s in range(v * per_wave, (v + 1) * per_wave):
                upto = first_from(s + 1, begins[s] + j * chunk)
                parts.append(jnp.where((lane >= s) & (lane < upto), 0.0, FAR))
            at = stale + v * fresh + j * rows
            bias[at : at + rows, :] = jnp.concatenate(parts, axis=0).astype(BF16)

    for c in own_scales:
        c.wait()

    def rms_heads(value, which):
        out = []
        for h in range(heads):
            part = value[:, h * head_dim : (h + 1) * head_dim]
            power = jnp.sum(part * part, axis=-1, keepdims=True) * (1.0 / head_dim)
            out.append(part * lax.rsqrt(power + 1e-06) * gain[which : which + 1, :])
        return jnp.concatenate(out, axis=-1).astype(BF16)

    def spread_out(v, query, key, value):
        kv[freshly(v, y), 0:feat] = rms_heads(key, 1)
        kv[freshly(v, y), feat : 2 * feat] = value.astype(BF16)
        for c in kv_copies[v]:
            c.start()
        qg[v, x] = rms_heads(query, 0)
        for c in q_copies[v]:
            c.start()

    @pl.when(sec == 0)
    def _():
        for d in range(1, nz):
            arrived(st_recv.at[z_at(d)], st_r.at[z_at(d)])
        middles = [st_recv[i, 0:1, :] for i in range(nz)]
        mean = sum(middles) * (1.0 / nz)
        square = sum(st_recv[i, 1:2, :] for i in range(nz))
        square += sum((m - mean) * (m - mean) for m in middles) * feat
        scale = lax.rsqrt(square * (1.0 / width) + 1e-06)
        line = lax.broadcasted_iota(jnp.int32, (8, head_dim), 0)
        value = jnp.where(line == 0, mean, jnp.where(line == 1, scale, 0.0))
        st_norm[...] = value
        st_all[y] = value
        for c in sn_copies:
            c.start()
        for d in range(1, ny):
            arrived(st_all.at[y_at(d)], sn_r.at[y_at(d)])
        value = st_all[...].reshape(8 * ny, head_dim)
        value = jnp.concatenate([value, jnp.zeros((head_dim - 8 * ny, head_dim), F32)], axis=0)
        stats = jnp.transpose(value)
        for v in range(waves):
            for i in range(ny):
                mean = stats[v * rows : (v + 1) * rows, 8 * i : 8 * i + 1]
                scale = stats[v * rows : (v + 1) * rows, 8 * i + 1 : 8 * i + 2]
                for b in range(hz):

                    @pl.when(jnp.logical_not(is_own(i, b)))
                    def _():
                        arrived(xr.at[v, i, b], x_r.at[v, i, b])

                    at = pl.ds(pl.multiple_of((y * hz + b) * feat, feat), feat)
                    value = (xr[v, i, b].astype(F32) - mean) * scale
                    value = value * (1.0 + mod[1, :, at]) + mod[0, :, at]
                    xe[v, i, :, b * feat : (b + 1) * feat] = value.astype(BF16)
            if v == 0:
                for d in range(1, nx):
                    arrived(wbuf.at[:, y, x_at(d)], w_r.at[x_at(d)])
                pl.semaphore_signal(go.at[0], inc=1, device_id=other, device_id_type=MESH)
            tokens = xe[v].reshape(ny * rows, hz * feat)
            for i in range(3):
                weights = wbuf[i, y].reshape(nx * w_rows, feat)
                value = jnp.dot(tokens, weights, preferred_element_type=F32)
                psend[v, :, :, i * feat : (i + 1) * feat] = value.astype(BF16).reshape(
                    ny, rows, feat
                )
            for c in p_copies[v]:
                c.start()
        for v in range(waves):
            value = psend[v, y].astype(F32)
            for d in range(1, ny):
                arrived(precv.at[v, y_at(d)], p_r.at[v, y_at(d)])
                value += precv[v, y_at(d)].astype(F32)
            spread_out(v, value[:, 0:feat], value[:, feat : 2 * feat], value[:, 2 * feat :])

    @pl.when(sec == 1)
    def _():
        for v in range(waves):
            for i in range(nz):
                arrived(xg.at[v, i], h_r.at[v, i])
            own[v] = xg[v, z]
            total = jnp.zeros((rows, feat), F32)
            for i in range(nz):
                total += xg[v, i].astype(F32)
            mean = jnp.sum(total, axis=-1, keepdims=True) * (1.0 / width)
            total = jnp.zeros((rows, feat), F32)
            for i in range(nz):
                diff = xg[v, i].astype(F32) - mean
                total += diff * diff
            scale = lax.rsqrt(jnp.sum(total, axis=-1, keepdims=True) * (1.0 / width) + 1e-06)
            for i in range(nz):
                at = slice(i * feat, (i + 1) * feat)
                value = (xg[v, i].astype(F32) - mean) * scale
                value = value * (1.0 + mod[1, :, at]) + mod[0, :, at]
                xn[v, :, at] = value.astype(BF16)
            parts = [None] * 3
            for i in (1, 0, 2):
                if v == 0:
                    for d in range(1, ny):
                        arrived(wbuf.at[i, y_at(d), :, upper], wc_r.at[i, y_at(d)])
                    for d in range(1, nx):
                        arrived(wbuf.at[i, :, x_at(d), lower], wd_r.at[i, x_at(d)])
                weights = wbuf[i].reshape(width, feat)
                parts[i] = jnp.dot(xn[v], weights, preferred_element_type=F32)
            spread_out(v, *parts)

    for d in range(1, ny):
        arrived(kv.at[cached(y_at(d)), :], c_r.at[y_at(d)])
    lane_all = lax.broadcasted_iota(jnp.int32, (nx * rows, head_dim), 1)
    lane_tok = lax.broadcasted_iota(jnp.int32, (tok, head_dim), 1)
    exponent = math.log2(math.e) / math.sqrt(head_dim)
    for v in range(waves):
        for d in range(1, ny):
            arrived(kv.at[freshly(v, y_at(d)), :], kv_r.at[v, y_at(d)])
        for d in range(1, nx):
            arrived(qg.at[v, x_at(d)], q_r.at[v, x_at(d)])

        if v == 0:

            @pl.when(sec == 0)
            def _():
                pl.semaphore_signal(go.at[1], inc=1, device_id=other, device_id_type=MESH)

        keys_now = stale + (v + 1) * fresh
        tags = [
            jnp.where(lane_tok == s, 1.0, 0.0) for s in range(v * per_wave, (v + 1) * per_wave)
        ]
        tags = jnp.concatenate(tags * nx, axis=0).astype(BF16)
        sums = jnp.zeros((nx * rows, head_dim), F32)
        for h in range(heads):
            at = slice(h * head_dim, (h + 1) * head_dim)
            queries = jnp.concatenate([qg[v, :, :, at].reshape(nx * rows, head_dim), tags], axis=1)
            keys = jnp.concatenate([kv[0:keys_now, at], bias[0:keys_now, :]], axis=1)
            scores = lax.dot_general(
                queries, keys, (((1,), (1,)), ((), ())), preferred_element_type=F32
            )
            weight = jnp.exp2(scores * exponent)
            denom = jnp.sum(weight, axis=-1, keepdims=True)
            values = kv[0:keys_now, feat + h * head_dim : feat + (h + 1) * head_dim]
            numer = jnp.dot(weight.astype(BF16), values, preferred_element_type=F32)
            nsend[v, :, :, at] = numer.astype(BF16).reshape(nx, rows, head_dim)
            high = denom.astype(BF16).astype(F32)
            sums = jnp.where(lane_all == 2 * h, high, sums)
            sums = jnp.where(lane_all == 2 * h + 1, denom - high, sums)
        nsend[v, :, :, feat:] = sums.astype(BF16).reshape(nx, rows, head_dim)
        for c in num_copies[v]:
            c.start()

    for v in range(waves):
        total = nsend[v, x].astype(F32)
        for d in range(1, nx):
            arrived(nrecv.at[v, x_at(d)], n_r.at[v, x_at(d)])
            total += nrecv[v, x_at(d)].astype(F32)
        parts = []
        for h in range(heads):
            at = feat + 2 * h
            denom = total[:, at : at + 1] + total[:, at + 1 : at + 2]
            parts.append(total[:, h * head_dim : (h + 1) * head_dim] / denom)
        ag[v, z] = jnp.concatenate(parts, axis=1).astype(BF16)
        for c in a_copies[v]:
            c.start()

    @pl.when(sec == 0)
    def _():
        pl.semaphore_signal(go.at[2], inc=1, device_id=other, device_id_type=MESH)

    def source(c):
        pos = c * chunk
        first_row = -waves * fresh - pad
        for s in range(steps):
            row = (s // per_wave) * fresh + (s % per_wave) * tok
            row += (pos - begins[s]) // chunk * rows
            first_row = jnp.where(covers(s, pos), row, first_row)
        return first_row

    in_row = lax.broadcasted_iota(jnp.int32, (pad, waves * fresh), 0)
    in_col = lax.broadcasted_iota(jnp.int32, (pad, waves * fresh), 1)
    picks = []
    for c in range(nx):
        hit = (in_col - in_row == source(y * nx + c)) & (in_row < tok)
        picks.append(jnp.where(hit, 1.0, 0.0).astype(BF16))
    pick = jnp.concatenate(picks, axis=0)
    value = jnp.dot(pick, kv[stale:, :], preferred_element_type=F32)
    rsend[...] = value.astype(BF16).reshape(nx, pad, 2 * feat)
    for c in r_copies:
        c.start()

    own_wo.wait()
    gate = mod[2, :, pl.ds(pl.multiple_of(z * feat, feat), feat)]
    results = []
    for v in range(waves):
        for d in range(1, nz):
            arrived(ag.at[v, z_at(d)], ag_r.at[v, z_at(d)])
        attended = jnp.concatenate([ag[v, i] for i in range(nz)], axis=1)
        result = jnp.dot(attended, wo_v[...], preferred_element_type=F32)
        result = (own[v].astype(F32) + gate * result).astype(BF16)
        done[v] = result
        results.append(result.astype(F32))

        @pl.when(sec == 0)
        def _():
            for c in next_x[v]:
                c.start()

    result = jnp.concatenate(results, axis=0)
    parts = [result[s * tok : (s + 1) * tok] for s in range(steps)]
    value = []
    for p in range(steps):
        chosen = parts[0]
        for s in range(1, steps):
            chosen = jnp.where(places[s] == p, parts[s], chosen)
        value.append(chosen)
    bo[...] = jnp.concatenate(value, axis=0).astype(BF16)

    for d in range(1, nx):
        arrived(rrecv.at[x_at(d)], r_r.at[x_at(d)])
    rrecv[x] = rsend[x]
    out_row = lax.broadcasted_iota(jnp.int32, (chunk, nx * pad), 0)
    out_col = lax.broadcasted_iota(jnp.int32, (chunk, nx * pad), 1)
    block = out_col // pad
    within = out_col - block * pad
    hit = (out_row == block * tok + within) & (within < tok)
    place = jnp.where(hit, 1.0, 0.0).astype(BF16)
    written_to = source(seq) >= 0
    value = jnp.dot(place, rrecv[...].reshape(nx * pad, 2 * feat), preferred_element_type=F32)
    value = jnp.where(written_to, value, kv[cached(y), :].astype(F32)).astype(BF16)
    nk[...] = value[:, 0:feat]
    nv[...] = value[:, feat:]

    @pl.when(sec == 0)
    def _():
        for c in first_st + sn_copies + w_copies + sum(next_x + p_copies, []):
            c.wait_send()
        for v in range(waves):
            for c in first_x[v][1:]:
                c.wait_send()

            @pl.when(hy != y)
            def _():
                first_x[v][0].wait_send()

    @pl.when(sec == 1)
    def _():
        for c in wa_copies + wb_copies + sum(wc_copies + wd_copies, []):
            c.wait_send()

    for c in cache_copies + r_copies + sum(q_copies + kv_copies + num_copies + a_copies, []):
        c.wait_send()


def write_kernel(*refs):
    half = len(refs) // 2
    for src, dst in zip(refs[:half], refs[half:]):
        dst[...] = src[...]


def written(*arrays):
    vmem = pl.BlockSpec(memory_space=pltpu.VMEM)
    return pl.pallas_call(
        write_kernel,
        name="write",
        out_shape=tuple(jax.ShapeDtypeStruct(a.shape, a.dtype) for a in arrays),
        in_specs=[vmem] * len(arrays),
        out_specs=(vmem,) * len(arrays),
        compiler_params=pltpu.CompilerParams(vmem_limit_bytes=60 << 20),
    )(*arrays)


def per_device(
    patches, cache_k, cache_v, w_qkv, w_out, modulation, qk_gain, patch_order, patch_start
):
    nz = lax.axis_size("head")
    ny = nx = square_side(lax.axis_size("seq"))
    count, tok, feat = patches.shape
    chunk = cache_k.shape[1]
    head_dim = qk_gain.shape[-1]
    waves = 2
    per_wave = count // waves
    rows = per_wave * tok
    hz = nz // ny
    w_rows = w_qkv.shape[1]
    pad = -(-tok // 16) * 16
    keys = ny * (waves * rows + chunk)
    dma = pltpu.SemaphoreType.DMA
    vmem = pl.BlockSpec(memory_space=pltpu.VMEM)
    hbm = pl.BlockSpec(memory_space=pl.ANY)
    out, new_k, new_v = pl.pallas_call(
        functools.partial(block_kernel, nz, ny, nx, tok, waves, per_wave, head_dim),
        name="blocks",
        out_shape=(
            jax.ShapeDtypeStruct((count * tok, feat), BF16),
            jax.ShapeDtypeStruct((chunk, feat), BF16),
            jax.ShapeDtypeStruct((chunk, feat), BF16),
        ),
        in_specs=[hbm] * 9,
        out_specs=(vmem, vmem, vmem),
        scratch_shapes=[
            pltpu.SMEM((count,), jnp.int32),
            pltpu.SMEM((count,), jnp.int32),
            pltpu.VMEM((3, 1, nz * feat), F32),
            pltpu.VMEM((2, head_dim), F32),
            pltpu.VMEM((count * tok, feat), BF16),
            pltpu.VMEM((waves, rows, feat), BF16),
            pltpu.VMEM((waves, rows, feat), BF16),
            pltpu.VMEM((waves, ny, hz, rows, feat), BF16),
            pltpu.VMEM((waves, ny, rows, hz * feat), BF16),
            pltpu.VMEM((waves, nz, rows, feat), BF16),
            pltpu.VMEM((waves, rows, nz * feat), BF16),
            pltpu.VMEM((8, head_dim), F32),
            pltpu.VMEM((nz, 8, head_dim), F32),
            pltpu.VMEM((8, head_dim), F32),
            pltpu.VMEM((ny, 8, head_dim), F32),
            pltpu.VMEM((3, ny, nx, w_rows, feat), BF16),
            pltpu.VMEM((nz * feat, feat), BF16),
            pltpu.VMEM((waves, ny, rows, 3 * feat), BF16),
            pltpu.VMEM((waves, ny, rows, 3 * feat), BF16),
            pltpu.VMEM((waves, nx, rows, feat), BF16),
            pltpu.VMEM((keys, 2 * feat), BF16),
            pltpu.VMEM((keys, head_dim), BF16),
            pltpu.VMEM((waves, nx, rows, feat + head_dim), BF16),
            pltpu.VMEM((waves, nx, rows, feat + head_dim), BF16),
            pltpu.VMEM((waves, nz, rows, feat), BF16),
            pltpu.VMEM((nx, pad, 2 * feat), BF16),
            pltpu.VMEM((nx, pad, 2 * feat), BF16),
            dma((9,)),
            dma((waves, nz)),
            dma((waves, ny, hz)),
            dma((nz,)),
            dma((nz,)),
            dma((ny,)),
            dma((ny,)),
            dma((waves, nz)),
            dma((waves, nz)),
            dma((nx,)),
            dma((nx,)),
            dma((nx,)),
            dma((nx,)),
            dma((ny,)),
            dma((ny,)),
            dma((3, ny)),
            dma((3, ny)),
            dma((3, nx)),
            dma((3, nx)),
            dma((ny,)),
            dma((ny,)),
            dma((waves, ny)),
            dma((waves, ny)),
            dma((waves, nx)),
            dma((waves, nx)),
            dma((waves, ny)),
            dma((waves, ny)),
            dma((waves, nx)),
            dma((waves, nx)),
            dma((waves, nz)),
            dma((waves, nz)),
            dma((nx,)),
            dma((nx,)),
            pltpu.SemaphoreType.REGULAR((3,)),
        ],
        compiler_params=pltpu.CompilerParams(
            collective_id=0, has_side_effects=True, vmem_limit_bytes=60 << 20
        ),
    )(
        patch_order,
        patch_start,
        patches.reshape(count * tok, feat),
        cache_k[0],
        cache_v[0],
        jnp.transpose(w_qkv[0], (1, 0, 2)),
        w_out[0],
        jnp.transpose(modulation, (1, 0, 2)),
        qk_gain[0],
    )
    out, new_k, new_v = written(out, new_k, new_v)
    return (out.reshape(1, count, tok, feat), new_k[None], new_v[None])


def solution(mesh):
    return jax.shard_map(
        per_device,
        mesh=mesh,
        in_specs=(
            P(None, "seq", "head"),
            P("section", "seq", "head"),
            P("section", "seq", "head"),
            P("section", "seq", None, "head"),
            P("section", None, "head"),
            P("section", None, None),
            P("section", None, None),
            P(),
            P(),
        ),
        out_specs=(
            P("section", None, "seq", "head"),
            P("section", "seq", "head"),
            P("section", "seq", "head"),
        ),
        check_vma=False,
    )
```

time: 94 us -> 85.3 us (0.907)
  Pallas kernels: 93.2 us -> 84.5 us
    pallas_call x1, Pallas kernels: 91.6 us -> 82.9 us  [per_device(): pl.pallas_call(functools.partial(block_kernel, nz, ny, nx, tok, waves, pe...]
where the time goes in v4:
time: 85.3 us; the launch traced here: 85.2 us
  Pallas kernels  84.5 us (99%)
    pallas_call x1, Pallas kernels, per_device(): pl.pallas_call(functools.partial(block_kernel, nz, ny, nx, tok, waves, pe...  82.9 us

profile of v4, /device:TPU:1, one launch (start us, length us, event | category | flops | bytes accessed | tf_op | source)
XLA Modules:
  0.0 85.2 jit_solution(12636306595093672734)
XLA Ops:
  0.6 82.9 %blocks.1 = (bf16[96,384]{1,0:T(8,128)(2,1)}, bf16[96,384]{1,0:T(8,128)(2,1)}, bf16[96,384]{1,0:T(8,128)(2,1)}) custom-call(s32[4]{0:T(128)} %order_h.1, s32[4]{0:T(128)} %start_h.1, bf16[96,384]{1,0:T(8,128)(2,1)} %bitcast.14, bf16[96,384]{1,0:T(8,128)(2,1)} %bitcast.15, bf16[96,384]{1,0:T(8,128)(2,1)} %bitcast.16, bf16[3,192,384]{2,1,0:T(8,128)(2,1)} %bitcast.13, ...), custom_call_target="tpu_custom_call" | custom-call | tf_op jit(solution)/shard_map/blocks/pallas_call | solution.py:678
  83.5 1.6 %write.1 = (bf16[96,384]{1,0:T(8,128)(2,1)}, bf16[96,384]{1,0:T(8,128)(2,1)}, bf16[96,384]{1,0:T(8,128)(2,1)}) custom-call(bf16[96,384]{1,0:T(8,128)(2,1)} %get-tuple-element.9.refs_0_, bf16[96,384]{1,0:T(8,128)(2,1)} %get-tuple-element.10.refs_1_, bf16[96,384]{1,0:T(8,128)(2,1)} %get-tuple-element.11.refs_2_), custom_call_target="tpu_custom_call" | custom-call | tf_op jit(solution)/shard_map/write/pallas_call | solution.py:650

commit v5 on v4

--- a/solution.py
+++ b/solution.py
@@ -139,6 +139,9 @@
         return (sec, z, y * nx + x_at(d))
 
     other = (1 - sec, z, seq)
+    z_order = sorted(range(1, nz), key=lambda d: -min(d, nz - d))
+    y_order = sorted(range(1, ny), key=lambda d: -min(d, ny - d))
+    x_order = sorted(range(1, nx), key=lambda d: -min(d, nx - d))
 
     def copy(src, dst, ss, rs, dev):
         return pltpu.make_async_remote_copy(
@@ -183,22 +186,22 @@
                 x_r.at[v, y, lax.rem(z, hz)],
                 (0, z_at(d), hy * nx + x),
             )
-            for d in range(nz)
+            for d in [0] + z_order
         ]
     )
     first_st = [
-        copy(st_send, st_recv.at[z], st_s.at[d], st_r.at[z], on_z(d)) for d in range(1, nz)
+        copy(st_send, st_recv.at[z], st_s.at[d], st_r.at[z], on_z(d)) for d in z_order
     ]
     next_x = by_wave(
         lambda v: [
             copy(done.at[v], xg.at[v, z], h_s.at[v, d], h_r.at[v, z], (1, z_at(d), seq))
-            for d in range(nz)
+            for d in [0] + z_order
         ]
     )
     sn_copies = [
-        copy(st_norm, st_all.at[y], sn_s.at[d], sn_r.at[y], on_y(d)) for d in range(1, ny)
+        copy(st_norm, st_all.at[y], sn_s.at[d], sn_r.at[y], on_y(d)) for d in y_order
     ]
-    w_copies = [copy(w_slot, w_slot, w_s.at[d], w_r.at[x], on_x(d)) for d in range(1, nx)]
+    w_copies = [copy(w_slot, w_slot, w_s.at[d], w_r.at[x], on_x(d)) for d in x_order]
     half = w_rows // 2
     upper, lower = pl.ds(0, half), pl.ds(half, half)
 
@@ -214,17 +217,17 @@
         w_gather(wbuf.at[i, :, x, lower], wd_s.at[i], wd_r.at[i], x, on_x, nx) for i in range(3)
     ]
     cache_slot = kv.at[cached(y), :]
-    cache_copies = [copy(cache_slot, cache_slot, c_s.at[d], c_r.at[y], on_y(d)) for d in range(1, ny)]
+    cache_copies = [copy(cache_slot, cache_slot, c_s.at[d], c_r.at[y], on_y(d)) for d in y_order]
     p_copies = by_wave(
         lambda v: [
             copy(psend.at[v, y_at(d)], precv.at[v, y], p_s.at[v, d], p_r.at[v, y], on_y(d))
-            for d in range(1, ny)
+            for d in y_order
         ]
     )
     q_copies = by_wave(
         lambda v: [
             copy(qg.at[v, x], qg.at[v, x], q_s.at[v, d], q_r.at[v, x], on_x(d))
-            for d in range(1, nx)
+            for d in x_order
         ]
     )
     kv_copies = by_wave(
@@ -236,23 +239,23 @@
                 kv_r.at[v, y],
                 on_y(d),
             )
-            for d in range(1, ny)
+            for d in y_order
         ]
     )
     num_copies = by_wave(
         lambda v: [
             copy(nsend.at[v, x_at(d)], nrecv.at[v, x], n_s.at[v, d], n_r.at[v, x], on_x(d))
-            for d in range(1, nx)
+            for d in x_order
         ]
     )
     a_copies = by_wave(
         lambda v: [
             copy(ag.at[v, z], ag.at[v, z], ag_s.at[v, d], ag_r.at[v, z], on_z(d))
-            for d in range(1, nz)
+            for d in z_order
         ]
     )
     r_copies = [
-        copy(rsend.at[x_at(d)], rrecv.at[x], r_s.at[d], r_r.at[x], on_x(d)) for d in range(1, nx)
+        copy(rsend.at[x_at(d)], rrecv.at[x], r_s.at[d], r_r.at[x], on_x(d)) for d in x_order
     ]
 
     @pl.when(sec == 0)
@@ -323,7 +326,8 @@
         shard_stats(value)
         st_recv[z] = st_send[...]
         pl.semaphore_wait(barrier, len(partners) + 2 * nz - jnp.where(hy == y, 1, 0))
-        for c in first_st:
+        own_w.wait()
+        for c in w_copies + first_st:
             c.start()
         for v in range(waves):
             for c in first_x[v][1:]:
@@ -337,13 +341,16 @@
             def _():
                 first_x[v][0].start()
 
-    own_w.wait()
+    @pl.when(sec == 1)
+    def _():
+        own_w.wait()
+
     for c in own_cache:
         c.wait()
 
     @pl.when(sec == 0)
     def _():
-        for c in w_copies + cache_copies:
+        for c in cache_copies:
             c.start()
 
     @pl.when(sec == 1)
@@ -360,10 +367,10 @@
             c.start()
         for d in range(1, nx):
             arrived(wbuf.at[:, y, x_at(d), upper], wa_r.at[x_at(d)])
-        for c in wd_copies[0]:
+        for c in wd_copies[2]:
             c.start()
         pl.semaphore_wait(go.at[1], 1)
-        for c in wc_copies[1] + wc_copies[0] + wc_copies[2] + wd_copies[2] + cache_copies:
+        for c in wc_copies[1] + wc_copies[2] + wc_copies[0] + wd_copies[0] + cache_copies:
             c.start()
         pl.semaphore_wait(go.at[2], 1)
 
@@ -401,11 +408,13 @@
             out.append(part * lax.rsqrt(power + 1e-06) * gain[which : which + 1, :])
         return jnp.concatenate(out, axis=-1).astype(BF16)
 
-    def spread_out(v, query, key, value):
+    def spread_keys(v, key, value):
         kv[freshly(v, y), 0:feat] = rms_heads(key, 1)
         kv[freshly(v, y), feat : 2 * feat] = value.astype(BF16)
         for c in kv_copies[v]:
             c.start()
+
+    def spread_queries(v, query):
         qg[v, x] = rms_heads(query, 0)
         for c in q_copies[v]:
             c.start()
@@ -462,7 +471,8 @@
             for d in range(1, ny):
                 arrived(precv.at[v, y_at(d)], p_r.at[v, y_at(d)])
                 value += precv[v, y_at(d)].astype(F32)
-            spread_out(v, value[:, 0:feat], value[:, feat : 2 * feat], value[:, 2 * feat :])
+            spread_keys(v, value[:, feat : 2 * feat], value[:, 2 * feat :])
+            spread_queries(v, value[:, 0:feat])
 
     @pl.when(sec == 1)
     def _():
@@ -485,7 +495,7 @@
                 value = value * (1.0 + mod[1, :, at]) + mod[0, :, at]
                 xn[v, :, at] = value.astype(BF16)
             parts = [None] * 3
-            for i in (1, 0, 2):
+            for i in (1, 2, 0):
                 if v == 0:
                     for d in range(1, ny):
                         arrived(wbuf.at[i, y_at(d), :, upper], wc_r.at[i, y_at(d)])
@@ -493,7 +503,9 @@
                         arrived(wbuf.at[i, :, x_at(d), lower], wd_r.at[i, x_at(d)])
                 weights = wbuf[i].reshape(width, feat)
                 parts[i] = jnp.dot(xn[v], weights, preferred_element_type=F32)
-            spread_out(v, *parts)
+                if i == 2:
+                    spread_keys(v, parts[1], parts[2])
+            spread_queries(v, parts[0])
 
     for d in range(1, ny):
         arrived(kv.at[cached(y_at(d)), :], c_r.at[y_at(d)])
@@ -576,14 +588,33 @@
     for c in r_copies:
         c.start()
 
+    def refresh():
+        for d in range(1, nx):
+            arrived(rrecv.at[x_at(d)], r_r.at[x_at(d)])
+        rrecv[x] = rsend[x]
+        out_row = lax.broadcasted_iota(jnp.int32, (chunk, nx * pad), 0)
+        out_col = lax.broadcasted_iota(jnp.int32, (chunk, nx * pad), 1)
+        block = out_col // pad
+        within = out_col - block * pad
+        hit = (out_row == block * tok + within) & (within < tok)
+        place = jnp.where(hit, 1.0, 0.0).astype(BF16)
+        written_to = source(seq) >= 0
+        value = jnp.dot(place, rrecv[...].reshape(nx * pad, 2 * feat), preferred_element_type=F32)
+        value = jnp.where(written_to, value, kv[cached(y), :].astype(F32)).astype(BF16)
+        nk[...] = value[:, 0:feat]
+        nv[...] = value[:, feat:]
+
+    pl.when(sec == 1)(refresh)
     own_wo.wait()
     gate = mod[2, :, pl.ds(pl.multiple_of(z * feat, feat), feat)]
     results = []
     for v in range(waves):
-        for d in range(1, nz):
-            arrived(ag.at[v, z_at(d)], ag_r.at[v, z_at(d)])
-        attended = jnp.concatenate([ag[v, i] for i in range(nz)], axis=1)
-        result = jnp.dot(attended, wo_v[...], preferred_element_type=F32)
+        result = jnp.zeros((rows, feat), F32)
+        for d in [0] + z_order[::-1]:
+            if d:
+                arrived(ag.at[v, z_at(d)], ag_r.at[v, z_at(d)])
+            at = pl.ds(pl.multiple_of(z_at(d) * feat, feat), feat)
+            result += jnp.dot(ag[v, z_at(d)], wo_v[at, :], preferred_element_type=F32)
         result = (own[v].astype(F32) + gate * result).astype(BF16)
         done[v] = result
         results.append(result.astype(F32))
@@ -603,20 +634,7 @@
         value.append(chosen)
     bo[...] = jnp.concatenate(value, axis=0).astype(BF16)
 
-    for d in range(1, nx):
-        arrived(rrecv.at[x_at(d)], r_r.at[x_at(d)])
-    rrecv[x] = rsend[x]
-    out_row = lax.broadcasted_iota(jnp.int32, (chunk, nx * pad), 0)
-    out_col = lax.broadcasted_iota(jnp.int32, (chunk, nx * pad), 1)
-    block = out_col // pad
-    within = out_col - block * pad
-    hit = (out_row == block * tok + within) & (within < tok)
-    place = jnp.where(hit, 1.0, 0.0).astype(BF16)
-    written_to = source(seq) >= 0
-    value = jnp.dot(place, rrecv[...].reshape(nx * pad, 2 * feat), preferred_element_type=F32)
-    value = jnp.where(written_to, value, kv[cached(y), :].astype(F32)).astype(BF16)
-    nk[...] = value[:, 0:feat]
-    nv[...] = value[:, feat:]
+    pl.when(sec == 0)(refresh)
 
     @pl.when(sec == 0)
     def _():

time: 85.3 us -> 82.3 us (0.965)
  Pallas kernels: 84.5 us -> 81.5 us
    pallas_call x1, Pallas kernels: 82.9 us -> 79.9 us  [per_device(): pl.pallas_call(functools.partial(block_kernel, nz, ny, nx, tok, waves, pe...]
where the time goes in v5:
time: 82.3 us; the launch traced here: 82.1 us
  Pallas kernels  81.5 us (99%)
    pallas_call x1, Pallas kernels, per_device(): pl.pallas_call(functools.partial(block_kernel, nz, ny, nx, tok, waves, pe...  79.9 us
    pallas_call x1, Pallas kernels, written(): pl.pallas_call(write_kernel, name='write', out_shape=tuple((jax.ShapeDtyp...  1.65 us

profile of v5, /device:TPU:1, one launch (start us, length us, event | category | flops | bytes accessed | tf_op | source)
XLA Modules:
  0.0 82.1 jit_solution(15439364723653534754)
XLA Ops:
  0.6 79.9 %blocks.1 = (bf16[96,384]{1,0:T(8,128)(2,1)}, bf16[96,384]{1,0:T(8,128)(2,1)}, bf16[96,384]{1,0:T(8,128)(2,1)}) custom-call(s32[4]{0:T(128)} %order_h.1, s32[4]{0:T(128)} %start_h.1, bf16[96,384]{1,0:T(8,128)(2,1)} %bitcast.14, bf16[96,384]{1,0:T(8,128)(2,1)} %bitcast.15, bf16[96,384]{1,0:T(8,128)(2,1)} %bitcast.16, bf16[3,192,384]{2,1,0:T(8,128)(2,1)} %bitcast.13, ...), custom_call_target="tpu_custom_call" | custom-call | tf_op jit(solution)/shard_map/blocks/pallas_call | solution.py:696
  80.5 1.6 %write.1 = (bf16[96,384]{1,0:T(8,128)(2,1)}, bf16[96,384]{1,0:T(8,128)(2,1)}, bf16[96,384]{1,0:T(8,128)(2,1)}) custom-call(bf16[96,384]{1,0:T(8,128)(2,1)} %get-tuple-element.9.refs_0_, bf16[96,384]{1,0:T(8,128)(2,1)} %get-tuple-element.10.refs_1_, bf16[96,384]{1,0:T(8,128)(2,1)} %get-tuple-element.11.refs_2_), custom_call_target="tpu_custom_call" | custom-call | tf_op jit(solution)/shard_map/write/pallas_call | solution.py:668

commit v6 on v5

--- a/solution.py
+++ b/solution.py
@@ -86,6 +86,10 @@
     wc_r,
     wd_s,
     wd_r,
+    we_s,
+    we_r,
+    wf_s,
+    wf_r,
     c_s,
     c_r,
     p_s,
@@ -210,12 +214,47 @@
 
     wa_copies = w_gather(wbuf.at[:, y, x, upper], wa_s, wa_r, x, on_x, nx)
     wb_copies = w_gather(wbuf.at[:, y, x, lower], wb_s, wb_r, y, on_y, ny)
-    wc_copies = [
-        w_gather(wbuf.at[i, y, :, upper], wc_s.at[i], wc_r.at[i], y, on_y, ny) for i in range(3)
-    ]
-    wd_copies = [
-        w_gather(wbuf.at[i, :, x, lower], wd_s.at[i], wd_r.at[i], x, on_x, nx) for i in range(3)
-    ]
+    def w_parts(view, ss, rs, fs, fr, at, to, count):
+        near = sorted({1, count - 1})
+        assert count in (2, 4)
+        mine = [
+            [copy(view(i, at(0)), view(i, at(0)), ss.at[i, d], rs.at[i, d], to(d)) for d in near]
+            for i in range(3)
+        ]
+
+        def came(i):
+            for d in near:
+                arrived(view(i, at(count - d)), rs.at[i, d])
+
+        onward = []
+        for i in range(3):
+            onward.append([])
+            for d in near if count == 4 else ():
+                part = view(i, at(count - d), d != 1)
+                onward[i].append(copy(part, part, fs.at[i, d], fr.at[i, d], to(d)))
+
+        def came_onward(i):
+            for d in near if count == 4 else ():
+                arrived(view(i, at(2), d != 1), fr.at[i, d])
+
+        return mine, came, onward, came_onward
+
+    def pick_shards(count, part):
+        middle = count // 2
+        return slice(None) if part is None else pl.ds(middle * part, middle)
+
+    def upper_view(i, j, part=None):
+        return wbuf.at[i, j, pick_shards(nx, part), upper]
+
+    def lower_view(i, j, part=None):
+        return wbuf.at[i, pick_shards(ny, part), j, lower]
+
+    wc_copies, wc_came, wc_onward, wc_done = w_parts(
+        upper_view, wc_s, wc_r, we_s, we_r, y_at, on_y, ny
+    )
+    wd_copies, wd_came, wd_onward, wd_done = w_parts(
+        lower_view, wd_s, wd_r, wf_s, wf_r, x_at, on_x, nx
+    )
     cache_slot = kv.at[cached(y), :]
     cache_copies = [copy(cache_slot, cache_slot, c_s.at[d], c_r.at[y], on_y(d)) for d in y_order]
     p_copies = by_wave(
@@ -367,12 +406,32 @@
             c.start()
         for d in range(1, nx):
             arrived(wbuf.at[:, y, x_at(d), upper], wa_r.at[x_at(d)])
-        for c in wd_copies[2]:
+        wd_came(1)
+        for c in wd_onward[1]:
             c.start()
         pl.semaphore_wait(go.at[1], 1)
-        for c in wc_copies[1] + wc_copies[2] + wc_copies[0] + wd_copies[0] + cache_copies:
+        for c in wc_copies[1]:
             c.start()
         pl.semaphore_wait(go.at[2], 1)
+        for c in wd_copies[2] + wc_copies[2] + wd_copies[0] + wc_copies[0]:
+            c.start()
+        wc_came(1)
+        for c in wc_onward[1]:
+            c.start()
+        wd_came(2)
+        for c in wd_onward[2]:
+            c.start()
+        wc_came(2)
+        for c in wc_onward[2]:
+            c.start()
+        wd_came(0)
+        for c in wd_onward[0]:
+            c.start()
+        wc_came(0)
+        for c in wc_onward[0]:
+            c.start()
+        for c in cache_copies:
+            c.start()
 
     def covers(s, pos):
         return (begins[s] <= pos) & (pos < begins[s] + span)
@@ -497,10 +556,8 @@
             parts = [None] * 3
             for i in (1, 2, 0):
                 if v == 0:
-                    for d in range(1, ny):
-                        arrived(wbuf.at[i, y_at(d), :, upper], wc_r.at[i, y_at(d)])
-                    for d in range(1, nx):
-                        arrived(wbuf.at[i, :, x_at(d), lower], wd_r.at[i, x_at(d)])
+                    wc_done(i)
+                    wd_done(i)
                 weights = wbuf[i].reshape(width, feat)
                 parts[i] = jnp.dot(xn[v], weights, preferred_element_type=F32)
                 if i == 2:
@@ -518,7 +575,7 @@
         for d in range(1, nx):
             arrived(qg.at[v, x_at(d)], q_r.at[v, x_at(d)])
 
-        if v == 0:
+        if v == waves - 1:
 
             @pl.when(sec == 0)
             def _():
@@ -549,6 +606,10 @@
         for c in num_copies[v]:
             c.start()
 
+    @pl.when(sec == 0)
+    def _():
+        pl.semaphore_signal(go.at[2], inc=1, device_id=other, device_id_type=MESH)
+
     for v in range(waves):
         total = nsend[v, x].astype(F32)
         for d in range(1, nx):
@@ -562,10 +623,6 @@
         ag[v, z] = jnp.concatenate(parts, axis=1).astype(BF16)
         for c in a_copies[v]:
             c.start()
-
-    @pl.when(sec == 0)
-    def _():
-        pl.semaphore_signal(go.at[2], inc=1, device_id=other, device_id_type=MESH)
 
     def source(c):
         pos = c * chunk
@@ -650,7 +707,7 @@
 
     @pl.when(sec == 1)
     def _():
-        for c in wa_copies + wb_copies + sum(wc_copies + wd_copies, []):
+        for c in wa_copies + wb_copies + sum(wc_copies + wd_copies + wc_onward + wd_onward, []):
             c.wait_send()
 
     for c in cache_copies + r_copies + sum(q_copies + kv_copies + num_copies + a_copies, []):
@@ -750,6 +807,10 @@
             dma((3, ny)),
             dma((3, nx)),
             dma((3, nx)),
+            dma((3, ny)),
+            dma((3, ny)),
+            dma((3, nx)),
+            dma((3, nx)),
             dma((ny,)),
             dma((ny,)),
             dma((waves, ny)),

time: 82.3 us -> 79.4 us (0.965)
  Pallas kernels: 81.5 us -> 78.6 us
    pallas_call x1, Pallas kernels: 79.9 us -> 77 us  [per_device(): pl.pallas_call(functools.partial(block_kernel, nz, ny, nx, tok, waves, pe...]
where the time goes in v6:
time: 79.4 us; the launch traced here: 79.3 us
  Pallas kernels  78.6 us (99%)
    pallas_call x1, Pallas kernels, per_device(): pl.pallas_call(functools.partial(block_kernel, nz, ny, nx, tok, waves, pe...  77 us
    pallas_call x1, Pallas kernels, written(): pl.pallas_call(write_kernel, name='write', out_shape=tuple((jax.ShapeDtyp...  1.65 us

profile of v6, /device:TPU:1, one launch (start us, length us, event | category | flops | bytes accessed | tf_op | source)
XLA Modules:
  0.0 79.3 jit_solution(7705239785166200565)
XLA Ops:
  0.6 77.0 %blocks.1 = (bf16[96,384]{1,0:T(8,128)(2,1)}, bf16[96,384]{1,0:T(8,128)(2,1)}, bf16[96,384]{1,0:T(8,128)(2,1)}) custom-call(s32[4]{0:T(128)} %order_h.1, s32[4]{0:T(128)} %start_h.1, bf16[96,384]{1,0:T(8,128)(2,1)} %bitcast.14, bf16[96,384]{1,0:T(8,128)(2,1)} %bitcast.15, bf16[96,384]{1,0:T(8,128)(2,1)} %bitcast.16, bf16[3,192,384]{2,1,0:T(8,128)(2,1)} %bitcast.13, ...), custom_call_target="tpu_custom_call" | custom-call | tf_op jit(solution)/shard_map/blocks/pallas_call | solution.py:753
  77.6 1.6 %write.1 = (bf16[96,384]{1,0:T(8,128)(2,1)}, bf16[96,384]{1,0:T(8,128)(2,1)}, bf16[96,384]{1,0:T(8,128)(2,1)}) custom-call(bf16[96,384]{1,0:T(8,128)(2,1)} %get-tuple-element.9.refs_0_, bf16[96,384]{1,0:T(8,128)(2,1)} %get-tuple-element.10.refs_1_, bf16[96,384]{1,0:T(8,128)(2,1)} %get-tuple-element.11.refs_2_), custom_call_target="tpu_custom_call" | custom-call | tf_op jit(solution)/shard_map/write/pallas_call | solution.py:725

commit v7 on v6

--- a/solution.py
+++ b/solution.py
@@ -387,11 +387,6 @@
     for c in own_cache:
         c.wait()
 
-    @pl.when(sec == 0)
-    def _():
-        for c in cache_copies:
-            c.start()
-
     @pl.when(sec == 1)
     def _():
         pl.semaphore_wait(barrier, len(partners))
@@ -495,6 +490,8 @@
             c.start()
         for d in range(1, ny):
             arrived(st_all.at[y_at(d)], sn_r.at[y_at(d)])
+        for c in cache_copies:
+            c.start()
         value = st_all[...].reshape(8 * ny, head_dim)
         value = jnp.concatenate([value, jnp.zeros((head_dim - 8 * ny, head_dim), F32)], axis=0)
         stats = jnp.transpose(value)
@@ -512,10 +509,10 @@
                     value = (xr[v, i, b].astype(F32) - mean) * scale
                     value = value * (1.0 + mod[1, :, at]) + mod[0, :, at]
                     xe[v, i, :, b * feat : (b + 1) * feat] = value.astype(BF16)
-            if v == 0:
-                for d in range(1, nx):
-                    arrived(wbuf.at[:, y, x_at(d)], w_r.at[x_at(d)])
-                pl.semaphore_signal(go.at[0], inc=1, device_id=other, device_id_type=MESH)
+        for d in range(1, nx):
+            arrived(wbuf.at[:, y, x_at(d)], w_r.at[x_at(d)])
+        pl.semaphore_signal(go.at[0], inc=1, device_id=other, device_id_type=MESH)
+        for v in range(waves):
             tokens = xe[v].reshape(ny * rows, hz * feat)
             for i in range(3):
                 weights = wbuf[i, y].reshape(nx * w_rows, feat)

time: 79.4 us -> 78.4 us (0.987)
  Pallas kernels: 78.6 us -> 77.6 us
    pallas_call x1, Pallas kernels: 77 us -> 76 us  [per_device(): pl.pallas_call(functools.partial(block_kernel, nz, ny, nx, tok, waves, pe...]
where the time goes in v7:
time: 78.4 us; the launch traced here: 78.3 us
  Pallas kernels  77.6 us (99%)
    pallas_call x1, Pallas kernels, per_device(): pl.pallas_call(functools.partial(block_kernel, nz, ny, nx, tok, waves, pe...  76 us
    pallas_call x1, Pallas kernels, written(): pl.pallas_call(write_kernel, name='write', out_shape=tuple((jax.ShapeDtyp...  1.65 us

profile of v7, /device:TPU:1, one launch (start us, length us, event | category | flops | bytes accessed | tf_op | source)
XLA Modules:
  0.0 78.3 jit_solution(4169833865779460777)
XLA Ops:
  0.6 76.0 %blocks.1 = (bf16[96,384]{1,0:T(8,128)(2,1)}, bf16[96,384]{1,0:T(8,128)(2,1)}, bf16[96,384]{1,0:T(8,128)(2,1)}) custom-call(s32[4]{0:T(128)} %order_h.1, s32[4]{0:T(128)} %start_h.1, bf16[96,384]{1,0:T(8,128)(2,1)} %bitcast.14, bf16[96,384]{1,0:T(8,128)(2,1)} %bitcast.15, bf16[96,384]{1,0:T(8,128)(2,1)} %bitcast.16, bf16[3,192,384]{2,1,0:T(8,128)(2,1)} %bitcast.13, ...), custom_call_target="tpu_custom_call" | custom-call | tf_op jit(solution)/shard_map/blocks/pallas_call | solution.py:750
  76.6 1.6 %write.1 = (bf16[96,384]{1,0:T(8,128)(2,1)}, bf16[96,384]{1,0:T(8,128)(2,1)}, bf16[96,384]{1,0:T(8,128)(2,1)}) custom-call(bf16[96,384]{1,0:T(8,128)(2,1)} %get-tuple-element.9.refs_0_, bf16[96,384]{1,0:T(8,128)(2,1)} %get-tuple-element.10.refs_1_, bf16[96,384]{1,0:T(8,128)(2,1)} %get-tuple-element.11.refs_2_), custom_call_target="tpu_custom_call" | custom-call | tf_op jit(solution)/shard_map/write/pallas_call | solution.py:722

commit v8 on v7

--- a/solution.py
+++ b/solution.py
@@ -37,6 +37,9 @@
     wo,
     mod_h,
     gain_h,
+    bo_h,
+    nk_h,
+    nv_h,
     bo,
     nk,
     nv,
@@ -177,6 +180,11 @@
         pltpu.make_async_copy(gain_h, gain, loc.at[7]),
     ]
     own_wo = pltpu.make_async_copy(wo, wo_v, loc.at[8])
+    out_cache = [
+        pltpu.make_async_copy(nk, nk_h, loc.at[9]),
+        pltpu.make_async_copy(nv, nv_h, loc.at[10]),
+    ]
+    out_block = pltpu.make_async_copy(bo, bo_h, loc.at[11])
 
     def by_wave(make):
         return [make(v) for v in range(waves)]
@@ -657,6 +665,8 @@
         value = jnp.where(written_to, value, kv[cached(y), :].astype(F32)).astype(BF16)
         nk[...] = value[:, 0:feat]
         nv[...] = value[:, feat:]
+        for c in out_cache:
+            c.start()
 
     pl.when(sec == 1)(refresh)
     own_wo.wait()
@@ -687,6 +697,7 @@
             chosen = jnp.where(places[s] == p, parts[s], chosen)
         value.append(chosen)
     bo[...] = jnp.concatenate(value, axis=0).astype(BF16)
+    out_block.start()
 
     pl.when(sec == 0)(refresh)
 
@@ -709,6 +720,8 @@
 
     for c in cache_copies + r_copies + sum(q_copies + kv_copies + num_copies + a_copies, []):
         c.wait_send()
+    for c in out_cache + [out_block]:
+        c.wait()
 
 
 def write_kernel(*refs):
@@ -745,7 +758,6 @@
     pad = -(-tok // 16) * 16
     keys = ny * (waves * rows + chunk)
     dma = pltpu.SemaphoreType.DMA
-    vmem = pl.BlockSpec(memory_space=pltpu.VMEM)
     hbm = pl.BlockSpec(memory_space=pl.ANY)
     out, new_k, new_v = pl.pallas_call(
         functools.partial(block_kernel, nz, ny, nx, tok, waves, per_wave, head_dim),
@@ -756,8 +768,11 @@
             jax.ShapeDtypeStruct((chunk, feat), BF16),
         ),
         in_specs=[hbm] * 9,
-        out_specs=(vmem, vmem, vmem),
+        out_specs=(hbm, hbm, hbm),
         scratch_shapes=[
+            pltpu.VMEM((count * tok, feat), BF16),
+            pltpu.VMEM((chunk, feat), BF16),
+            pltpu.VMEM((chunk, feat), BF16),
             pltpu.SMEM((count,), jnp.int32),
             pltpu.SMEM((count,), jnp.int32),
             pltpu.VMEM((3, 1, nz * feat), F32),
@@ -785,7 +800,7 @@
             pltpu.VMEM((waves, nz, rows, feat), BF16),
             pltpu.VMEM((nx, pad, 2 * feat), BF16),
             pltpu.VMEM((nx, pad, 2 * feat), BF16),
-            dma((9,)),
+            dma((12,)),
             dma((waves, nz)),
             dma((waves, ny, hz)),
             dma((nz,)),

time: 78.4 us -> 78.2 us (level)
  no operation moved by 1% of the time
where the time goes in v8:
time: 78.2 us; the launch traced here: 78.1 us
  Pallas kernels  77.4 us (99%)
    pallas_call x1, Pallas kernels, per_device(): pl.pallas_call(functools.partial(block_kernel, nz, ny, nx, tok, waves, pe...  75.8 us
    pallas_call x1, Pallas kernels, written(): pl.pallas_call(write_kernel, name='write', out_shape=tuple((jax.ShapeDtyp...  1.65 us

profile of v8, /device:TPU:1, one launch (start us, length us, event | category | flops | bytes accessed | tf_op | source)
XLA Modules:
  0.0 78.1 jit_solution(8226493772341283572)
XLA Ops:
  0.6 75.8 %blocks.1 = (bf16[96,384]{1,0:T(8,128)(2,1)}, bf16[96,384]{1,0:T(8,128)(2,1)}, bf16[96,384]{1,0:T(8,128)(2,1)}) custom-call(s32[4]{0:T(128)} %order_h.1, s32[4]{0:T(128)} %start_h.1, bf16[96,384]{1,0:T(8,128)(2,1)} %bitcast.14, bf16[96,384]{1,0:T(8,128)(2,1)} %bitcast.15, bf16[96,384]{1,0:T(8,128)(2,1)} %bitcast.16, bf16[3,192,384]{2,1,0:T(8,128)(2,1)} %bitcast.13, ...), custom_call_target="tpu_custom_call" | custom-call | tf_op jit(solution)/shard_map/blocks/pallas_call | solution.py:762
  76.4 1.6 %write.1 = (bf16[96,384]{1,0:T(8,128)(2,1)}, bf16[96,384]{1,0:T(8,128)(2,1)}, bf16[96,384]{1,0:T(8,128)(2,1)}) custom-call(bf16[96,384]{1,0:T(8,128)(2,1)} %get-tuple-element.9.refs_0_, bf16[96,384]{1,0:T(8,128)(2,1)} %get-tuple-element.10.refs_1_, bf16[96,384]{1,0:T(8,128)(2,1)} %get-tuple-element.11.refs_2_), custom_call_target="tpu_custom_call" | custom-call | tf_op jit(solution)/shard_map/write/pallas_call | solution.py:735
